TPU v7x, 32 devices: a whole 2x2x4 slice. The times are simulated.
32 devices in a mesh: replica: 8 (over z, x), shard: 4 (over y, core).
Axes of the slice: x: 2, y: 2, z: 4, core: 2. Of those that a mesh axis runs over, the one named last changes fastest.
Arguments:
- images: bfloat16 [96, 197, 384], P(('replica', 'shard')), may hold values from -6 to 6
- counts: int32 [32], P(('replica', 'shard')), may hold values from 1 to 3, 51 in all
- first_gain: bfloat16 [384], P('shard'), may hold values from 0.25 to 1.75
- first_shift: bfloat16 [384], P('shard'), may hold values from -3 to 3
- project_in: bfloat16 [384, 1152], P('shard'), may hold values from -0.4375 to 0.4375
- query_bias: bfloat16 [384], P('shard'), may hold values from -3 to 3
- value_bias: bfloat16 [384], P('shard'), may hold values from -3 to 3
- project_out: bfloat16 [384, 384], P('shard'), may hold values from -0.875 to 0.875
- output_bias: bfloat16 [384], P('shard'), may hold values from -3 to 3
- second_gain: bfloat16 [384], P('shard'), may hold values from 0.25 to 1.75
- second_shift: bfloat16 [384], P('shard'), may hold values from -3 to 3
- expand_weight: bfloat16 [384, 1536], P('shard'), may hold values from -0.3125 to 0.3125
- expand_bias: bfloat16 [1536], P('shard'), may hold values from -3 to 3
- reduce_weight: bfloat16 [1536, 384], P('shard'), may hold values from -0.21875 to 0.21875
- reduce_bias: bfloat16 [384], P('shard'), may hold values from -3 to 3
- cotangent: bfloat16 [96, 197, 384], P(('replica', 'shard')), may hold values from -6 to 6
Outputs:
- output: bfloat16 [96, 197, 384], P(('replica', 'shard'))
- input_grad: bfloat16 [96, 197, 384], P(('replica', 'shard'))
- first_gain_grad: float32 [384], P('shard')
- first_shift_grad: float32 [384], P('shard')
- project_in_grad: float32 [384, 1152], P('shard')
- query_bias_grad: float32 [384], P('shard')
- value_bias_grad: float32 [384], P('shard')
- project_out_grad: float32 [384, 384], P('shard')
- output_bias_grad: float32 [384], P('shard')
- second_gain_grad: float32 [384], P('shard')
- second_shift_grad: float32 [384], P('shard')
- expand_weight_grad: float32 [384, 1536], P('shard')
- expand_bias_grad: float32 [1536], P('shard')
- reduce_weight_grad: float32 [1536, 384], P('shard')
- reduce_bias_grad: float32 [384], P('shard')
Inputs may be any that keep to these rules, and one draw needn't show every extreme that they name: Device d holds counts[d] real images in its first slots; the counts sum to 51 and some device's count is 3.
All inputs are finite; a program needn't handle non-finite values.
Results may differ from a plain program's by a relative error of at most 0.012.
The roundings to bfloat16 on the way count: a program that leaves them out, or rounds other values in their place, can miss the bound.
Values may be sent and summed in bfloat16 or wider, within the bound.
A program may use at most 128 MiB of HBM per device.

v0:
```python
import jax
import jax.numpy as jnp
from jax import lax
from jax.sharding import PartitionSpec as P

HEADS = 6
HEAD_DIM = 64


EPS = 1e-06


def layer_norm(hidden_rows, gain_vector, shift_vector):
    center = hidden_rows - jnp.mean(hidden_rows, -1, keepdims=True)
    spread = jnp.mean(center * center, -1, keepdims=True)
    return center * lax.rsqrt(spread + EPS) * gain_vector + shift_vector


def gelu_exact(argument):
    return jax.nn.gelu(argument, approximate=False)


def column_total(gradient):
    return jnp.sum(gradient.astype(jnp.float32), axis=0)


def outer_sum(left, right):
    return lax.dot_general(
        left, right, (((0,), (0,)), ((), ())), preferred_element_type=jnp.float32
    )


def back_product(gradient, weight):
    return lax.dot_general(
        gradient, weight, (((1,), (1,)), ((), ())), preferred_element_type=jnp.float32
    )


def attend_scores(queries, key_rows, score_scale):
    return (
        jnp.einsum("sqhd,skhd->shqk", queries, key_rows, preferred_element_type=jnp.float32)
        * score_scale
    )


def body(
    images,
    counts,
    first_gain,
    first_shift,
    project_in,
    query_bias,
    value_bias,
    project_out,
    output_bias,
    second_gain,
    second_shift,
    expand_weight,
    expand_bias,
    reduce_weight,
    reduce_bias,
    cotangent,
):
    slot_count, length, feature_width = images.shape
    score_scale = HEAD_DIM ** (-0.5)
    head_shape = (slot_count, length, HEADS, HEAD_DIM)
    gathered = (
        lax.all_gather(first_gain, "shard", axis=0, tiled=True),
        lax.all_gather(first_shift, "shard", axis=0, tiled=True),
        lax.all_gather(project_in, "shard", axis=0, tiled=True),
        lax.all_gather(query_bias, "shard", axis=0, tiled=True),
        lax.all_gather(value_bias, "shard", axis=0, tiled=True),
        lax.all_gather(project_out, "shard", axis=0, tiled=True),
        lax.all_gather(output_bias, "shard", axis=0, tiled=True),
        lax.all_gather(second_gain, "shard", axis=0, tiled=True),
        lax.all_gather(second_shift, "shard", axis=0, tiled=True),
        lax.all_gather(expand_weight, "shard", axis=0, tiled=True),
        lax.all_gather(expand_bias, "shard", axis=0, tiled=True),
        lax.all_gather(reduce_weight, "shard", axis=0, tiled=True),
        lax.all_gather(reduce_bias, "shard", axis=0, tiled=True),
    )
    (
        gain_one,
        shift_one,
        inproj_full,
        query_shift,
        value_shift,
        outproj_full,
        out_shift,
        gain_two,
        shift_two,
        expand_full,
        expand_shift,
        reduce_full,
        reduce_shift,
    ) = gathered
    gain_one = gain_one.astype(jnp.float32)
    gain_two = gain_two.astype(jnp.float32)
    alive = (jnp.arange(slot_count) < counts[0]).astype(jnp.float32)
    tokens = images.astype(jnp.float32).reshape(-1, feature_width)
    normed_one = layer_norm(tokens, gain_one, shift_one.astype(jnp.float32)).astype(jnp.bfloat16)
    triple = jnp.dot(normed_one, inproj_full, preferred_element_type=jnp.float32)
    queries = (
        (triple[:, :feature_width] + query_shift.astype(jnp.float32))
        .astype(jnp.bfloat16)
        .reshape(head_shape)
    )
    key_rows = triple[:, feature_width : 2 * feature_width].astype(jnp.bfloat16).reshape(head_shape)
    value_rows = (
        (triple[:, 2 * feature_width :] + value_shift.astype(jnp.float32))
        .astype(jnp.bfloat16)
        .reshape(head_shape)
    )
    scores = attend_scores(queries, key_rows, score_scale)
    row_max = jnp.max(scores, -1, keepdims=True)
    log_total = row_max + jnp.log(jnp.sum(jnp.exp(scores - row_max), -1, keepdims=True))
    attend_weights = jnp.exp(scores - log_total).astype(jnp.bfloat16)
    mixed = jnp.einsum(
        "shqk,skhd->sqhd", attend_weights, value_rows, preferred_element_type=jnp.float32
    )
    mixed = mixed.reshape(-1, feature_width).astype(jnp.bfloat16)
    middle = (
        tokens
        + jnp.dot(mixed, outproj_full, preferred_element_type=jnp.float32)
        + out_shift.astype(jnp.float32)
    )
    normed_two = layer_norm(middle, gain_two, shift_two.astype(jnp.float32)).astype(jnp.bfloat16)
    before_gelu = jnp.dot(
        normed_two, expand_full, preferred_element_type=jnp.float32
    ) + expand_shift.astype(jnp.float32)
    hidden = gelu_exact(before_gelu).astype(jnp.bfloat16)
    result = (
        middle
        + jnp.dot(hidden, reduce_full, preferred_element_type=jnp.float32)
        + reduce_shift.astype(jnp.float32)
    )
    output = (result.reshape(slot_count, length, feature_width) * alive[:, None, None]).astype(
        jnp.bfloat16
    )
    reduce_back, expand_back, gain_two_back, outproj_back, inproj_back, gain_one_back = (
        lax.all_gather(reduce_weight, "shard", axis=0, tiled=True),
        lax.all_gather(expand_weight, "shard", axis=0, tiled=True),
        lax.all_gather(second_gain, "shard", axis=0, tiled=True),
        lax.all_gather(project_out, "shard", axis=0, tiled=True),
        lax.all_gather(project_in, "shard", axis=0, tiled=True),
        lax.all_gather(first_gain, "shard", axis=0, tiled=True),
    )
    gain_two_back = gain_two_back.astype(jnp.float32)
    gain_one_back = gain_one_back.astype(jnp.float32)
    out_grad = (cotangent.astype(jnp.float32) * alive[:, None, None]).reshape(-1, feature_width)
    branch_grad = out_grad.astype(jnp.bfloat16)
    reduce_weight_grad = outer_sum(hidden, branch_grad)
    reduce_bias_grad = column_total(branch_grad)
    hidden_grad = back_product(branch_grad, reduce_back)
    _, gelu_pull = jax.vjp(gelu_exact, before_gelu)
    expand_grad = gelu_pull(hidden_grad)[0].astype(jnp.bfloat16)
    expand_weight_grad = outer_sum(normed_two, expand_grad)
    expand_bias_grad = column_total(expand_grad)
    normed_two_grad = back_product(expand_grad, expand_back)
    _, norm_two_pull = jax.vjp(layer_norm, middle, gain_two_back, jnp.zeros_like(gain_two_back))
    middle_norm_grad, second_gain_grad, second_shift_grad = norm_two_pull(normed_two_grad)
    middle_grad = out_grad + middle_norm_grad
    proj_grad = middle_grad.astype(jnp.bfloat16)
    project_out_grad = outer_sum(mixed, proj_grad)
    output_bias_grad = column_total(proj_grad)
    mixed_grad = back_product(proj_grad, outproj_back).astype(jnp.bfloat16).reshape(head_shape)
    scores_again = attend_scores(queries, key_rows, score_scale)
    probs_exact = jnp.exp(scores_again - log_total)
    probs_round = probs_exact.astype(jnp.bfloat16)
    values_grad = jnp.einsum(
        "shqk,sqhd->skhd", probs_round, mixed_grad, preferred_element_type=jnp.float32
    )
    probs_grad = jnp.einsum(
        "sqhd,skhd->shqk", mixed_grad, value_rows, preferred_element_type=jnp.float32
    )
    scores_grad = probs_exact * (probs_grad - jnp.sum(probs_exact * probs_grad, -1, keepdims=True))
    scores_grad = scores_grad.astype(jnp.bfloat16)
    queries_grad = (
        jnp.einsum("shqk,skhd->sqhd", scores_grad, key_rows, preferred_element_type=jnp.float32)
        * score_scale
    )
    keys_grad = (
        jnp.einsum("shqk,sqhd->skhd", scores_grad, queries, preferred_element_type=jnp.float32)
        * score_scale
    )
    triple_grad = jnp.concatenate(
        (
            queries_grad.reshape(-1, feature_width),
            keys_grad.reshape(-1, feature_width),
            values_grad.reshape(-1, feature_width),
        ),
        axis=1,
    ).astype(jnp.bfloat16)
    project_in_grad = outer_sum(normed_one, triple_grad)
    query_bias_grad = column_total(triple_grad[:, :feature_width])
    value_bias_grad = column_total(triple_grad[:, 2 * feature_width :])
    normed_one_grad = back_product(triple_grad, inproj_back)
    _, norm_one_pull = jax.vjp(layer_norm, tokens, gain_one_back, jnp.zeros_like(gain_one_back))
    tokens_norm_grad, first_gain_grad, first_shift_grad = norm_one_pull(normed_one_grad)
    input_grad = (
        (middle_grad + tokens_norm_grad)
        .reshape(slot_count, length, feature_width)
        .astype(jnp.bfloat16)
    )
    shares = (
        lax.psum_scatter(first_gain_grad, "shard", scatter_dimension=0, tiled=True),
        lax.psum_scatter(first_shift_grad, "shard", scatter_dimension=0, tiled=True),
        lax.psum_scatter(project_in_grad, "shard", scatter_dimension=0, tiled=True),
        lax.psum_scatter(query_bias_grad, "shard", scatter_dimension=0, tiled=True),
        lax.psum_scatter(value_bias_grad, "shard", scatter_dimension=0, tiled=True),
        lax.psum_scatter(project_out_grad, "shard", scatter_dimension=0, tiled=True),
        lax.psum_scatter(output_bias_grad, "shard", scatter_dimension=0, tiled=True),
        lax.psum_scatter(second_gain_grad, "shard", scatter_dimension=0, tiled=True),
        lax.psum_scatter(second_shift_grad, "shard", scatter_dimension=0, tiled=True),
        lax.psum_scatter(expand_weight_grad, "shard", scatter_dimension=0, tiled=True),
        lax.psum_scatter(expand_bias_grad, "shard", scatter_dimension=0, tiled=True),
        lax.psum_scatter(reduce_weight_grad, "shard", scatter_dimension=0, tiled=True),
        lax.psum_scatter(reduce_bias_grad, "shard", scatter_dimension=0, tiled=True),
    )
    totals = tuple(
        lax.psum(
            (
                shares[0],
                shares[1],
                shares[2],
                shares[3],
                shares[4],
                shares[5],
                shares[6],
                shares[7],
                shares[8],
                shares[9],
                shares[10],
                shares[11],
                shares[12],
            ),
            "replica",
        )
    )
    return (
        output,
        input_grad,
        totals[0],
        totals[1],
        totals[2],
        totals[3],
        totals[4],
        totals[5],
        totals[6],
        totals[7],
        totals[8],
        totals[9],
        totals[10],
        totals[11],
        totals[12],
    )


def solution(mesh):
    return jax.shard_map(
        body,
        mesh=mesh,
        in_specs=(
            P(("replica", "shard"), None, None),
            P(("replica", "shard")),
            P("shard"),
            P("shard"),
            P("shard", None),
            P("shard"),
            P("shard"),
            P("shard", None),
            P("shard"),
            P("shard"),
            P("shard"),
            P("shard", None),
            P("shard"),
            P("shard", None),
            P("shard"),
            P(("replica", "shard"), None, None),
        ),
        out_specs=(
            P(("replica", "shard"), None, None),
            P(("replica", "shard"), None, None),
            P("shard"),
            P("shard"),
            P("shard", None),
            P("shard"),
            P("shard"),
            P("shard", None),
            P("shard"),
            P("shard"),
            P("shard"),
            P("shard", None),
            P("shard"),
            P("shard", None),
            P("shard"),
        ),
        check_vma=False,
    )
```

profile of v0, /device:TPU:0, one launch (start us, length us, event | category | flops | bytes accessed | tf_op | source)
XLA Modules:
  0.0 347.7 jit_solution(13367742385135492244)
XLA Ops:
  7.2 0.7 all-gather.4.cloned.1.call-update
  8.0 0.7 all-gather.6.cloned.1.call-update
  8.7 1.1 reshape.170
  9.8 1.2 convert_reduce_fusion.5
  11.1 1.3 multiply_reduce_fusion.2
  13.2 1.3 fusion.33
  15.1 0.9 dynamic-update-slice.1
  16.0 0.8 dynamic-update-slice
  16.9 0.8 dynamic-update-slice.2
  17.7 0.8 dynamic-update-slice.3
  18.6 0.8 dynamic-update-slice.4
  19.4 0.8 dynamic-update-slice.6
  20.3 0.8 dynamic-update-slice.5
  21.1 0.8 dynamic-update-slice.7
  22.0 8.5 %all-reduce.20 = (bf16[384]{0:T(512)(128)(2,1)S(1)}, bf16[384]{0:T(512)(128)(2,1)S(1)}, bf16[384]{0:T(512)(128)(2,1)S(1)}, bf16[384]{0:T(512)(128)(2,1)S(1)}, bf...) all-reduce(bf16[384]{0:T(512)(128)(2,1)S(1)} %dynamic-update-slice., ...), channel_id=1, replica_groups=mesh['replica'=8,'shard'=4] {'shard'}, use_global_device_ids=true, to_apply=%add.1 | all-reduce | flops 3072 | bytes 12288
  30.5 8.6 %all_gather.47 = bf16[384,1152]{1,0:T(8,128)(2,1)S(1)} all-gather(bf16[96,1152]{1,0:T(8,128)(2,1)} %param.20), channel_id=1, replica_groups=mesh['replica'=8,'shard'=4] {'shard'}, dimensions={0}, use_global_device_ids=true | all-gather | bytes 1105920 | tf_op jit(solution)/shard_map/all_gather | solution.py:70
  39.2 1.0 fusion.27
  40.2 0.8 slice.25
  41.0 0.9 fusion.15
  42.6 1.1 copy.68
  43.7 1.7 reshape.233
  45.5 1.1 copy.66
  46.6 2.7 reshape.234
  49.3 1.8 copy.67
  51.1 0.7 multiply_reduce_fusion.1
  51.9 0.7 exponential_reduce_fusion
  52.6 0.8 fusion.13
  54.6 6.1 %all_gather.50 = bf16[384,384]{1,0:T(8,128)(2,1)S(1)} all-gather(bf16[96,384]{1,0:T(8,128)(2,1)S(1)} %copy-done.22), channel_id=1, replica_groups=mesh['replica'=8,'shard'=4] {'shard'}, dimensions={0}, use_global_device_ids=true | all-gather | bytes 368640 | tf_op jit(solution)/shard_map/all_gather | solution.py:73
  60.7 5.3 %all-gather = bf16[4,1,384]{2,1,0:T(2,128)(2,1)S(1)} all-gather(bf16[1,1,384]{2,1,0:T(2,128)(2,1)S(1)} %reshape.204), channel_id=1, replica_groups=mesh['replica'=8,'shard'=4] {'shard'}, dimensions={0}, use_global_device_ids=true | all-gather | bytes 3840 | tf_op jit(solution)/shard_map/all_gather | solution.py:78
  67.0 12.0 %multiply_convert_fusion.1 = (bf16[591,1536]{1,0:T(8,128)(2,1)}, f32[591,1536]{1,0:T(8,128)}, f32[591,1536]{1,0:T(8,128)}) fusion(f32[1536]{0:T(1024)S(1)} %reshape.206, bf16[384,1536]{1,0:T(8,128)(2,1)} %all-gather.4.cloned.1.call-done, f32[591,384]{1,0:T(8,128)S(1)} %get-tuple-element.69, f32[384]{0:T(512)S(1)} %convert_element_type.129, ...), kind=kOutput, calls=%fused_computation.8 | convolution fusion | flops 758219904 | bytes 11179128 | tf_op jit(solution)/shard_map/dot_general | solution.py:128
  79.0 3.9 %fusion.10 = f32[591,384]{1,0:T(8,128)} fusion(f32[591,384]{1,0:T(8,128)S(1)} %get-tuple-element.69, bf16[591,1536]{1,0:T(8,128)(2,1)} %get-tuple-element.57, bf16[1536,384]{1,0:T(8,128)(2,1)} %all-gather.6.cloned.1.call-done, f32[384]{0:T(512)S(1)} %convert_element_type.133), kind=kOutput, calls=%fused_computation.36 | convolution fusion | flops 697625856 | bytes 4812288 | tf_op jit(solution)/shard_map/dot_general | solution.py:134
  82.9 1.3 reshape.174
  84.2 2.3 convert_reduce_fusion.3
  86.5 1.3 reshape.175
  87.8 5.9 %convert_reduce_fusion = (f32[1536]{0:T(1024)S(1)}, bf16[591,1536]{1,0:T(8,128)(2,1)S(1)}) fusion(f32[591,1536]{1,0:T(8,128)} %get-tuple-element.58, f32[591,1536]{1,0:T(8,128)} %get-tuple-element.70, bf16[1536,384]{1,0:T(8,128)(2,1)} %all-gather.6.cloned.1.call-done, f32[591,384]{1,0:T(8,128)S(1)} %reshape.175), kind=kOutput, calls=%fused_computation.6 | convolution fusion | flops 711921792 | bytes 11171328 | tf_op jit(solution)/shard_map/dot_general | solution.py:34
  93.8 1.3 multiply_reduce_fusion.3
  95.8 0.8 copy-done.6
  96.6 1.3 convolution_convert_fusion.2
  97.9 1.3 fusion.35
  99.1 1.7 reshape.235
  100.9 1.1 copy.72
  102.0 3.4 multiply_reduce_fusion
  105.4 0.8 multiply_convert_fusion
  106.5 1.3 fusion.12
  108.1 2.6 fusion.11
  110.7 1.6 copy.76
  112.7 1.8 copy.79
  114.9 3.0 fusion.14
  119.1 1.2 copy-done.21
  120.3 2.5 fusion.26
  122.9 4.2 %fusion.28 = f32[384,1536]{1,0:T(8,128)} fusion(bf16[591,1536]{1,0:T(8,128)(2,1)} %copy-done.25, f32[591,384]{1,0:T(8,128)S(1)} %copy-done.5, f32[384]{0:T(512)S(1)} %convert_element_type.129, f32[384]{0:T(512)S(1)} %convert_element_type.128, f32[591]{0:T(1024)S(1)} %fusion.23, f32[591]{0:T(1024)S(1)} %broadcast_multiply_fusion), kind=kOutput, calls=%fused_computation.87 | convolution fusion | flops 698306688 | bytes 5090424 | tf_op jit(solution)/shard_map/dot_general | solution.py:28
  127.2 4.2 %fusion.19 = f32[1536,384]{1,0:T(8,128)} fusion(bf16[591,1536]{1,0:T(8,128)(2,1)} %get-tuple-element.57, f32[591,384]{1,0:T(8,128)S(1)} %copy-done.3), kind=kOutput, calls=%fused_computation.64 | convolution fusion | flops 697398912 | bytes 5082624 | tf_op jit(solution)/shard_map/dot_general | solution.py:28
  131.5 31.4 %reduce-scatter.5.cloned.1.call-done = f32[96,1152]{1,0:T(8,128)} async-done(((f32[384,1152]{1,0:T(8,128)}), f32[96,1152]{1,0:T(8,128)}) %reduce-scatter.5.cloned.1.call-update) | async-done | bytes 442384 | tf_op jit(solution)/shard_map/reduce_scatter | solution.py:208
  162.9 35.6 %reduce-scatter.9.cloned.1.call-done = f32[96,1536]{1,0:T(8,128)} async-done(((f32[384,1536]{1,0:T(8,128)}), f32[96,1536]{1,0:T(8,128)}) %reduce-scatter.9.cloned.1.call-update) | async-done | bytes 589840 | tf_op jit(solution)/shard_map/reduce_scatter | solution.py:215
  198.5 35.5 %reduce-scatter.11.cloned.1.call-done = f32[384,384]{1,0:T(8,128)} async-done(((f32[1536,384]{1,0:T(8,128)}), f32[384,384]{1,0:T(8,128)}) %reduce-scatter.11.cloned.1.call-update) | async-done | bytes 589840 | tf_op jit(solution)/shard_map/reduce_scatter | solution.py:217
  235.4 2.7 multiply_reduce_fusion.4
  238.8 0.9 convert_element_type.143
  240.0 10.6 %all-reduce.19 = (f32[384]{0:T(512)S(1)}, f32[384]{0:T(512)S(1)}, f32[384]{0:T(512)S(1)}, f32[384]{0:T(512)S(1)}, f32[384]{0:T(512)S(1)}, /*index=5*/f32[384]{0:...) all-reduce(f32[384]{0:T(512)S(1)} %get-tuple-element.17, ...), channel_id=2, replica_groups=mesh['replica'=8,'shard'=4] {'shard'}, use_global_device_ids=true, to_apply=%region_12.0.clone | all-reduce | flops 4608 | bytes 36864
  251.3 23.0 %all-reduce.17 = (f32[96]{0:T(128)}, f32[96]{0:T(128)}, f32[96]{0:T(128)}, f32[96]{0:T(128)}, f32[96]{0:T(128)}, /*index=5*/f32[96]{0:T(128)}, f32[96]{0:T(128)}, f32[384]{0:T(512)}, f32[96]{0:T(128)}) all-reduce(f32[96]{0:T(128)S(1)} %dynamic-slice.9, f32[96]{0:T(128)S(1)} %dynamic-slice.11, ...), channel_id=1, replica_groups=mesh['replica'=8,'shard'=4] {'replica'}, use_global_device_ids=true, to_apply=%region_13.0 | all-reduce | flops 1152 | bytes 9216 | tf_op jit(solution)/shard_map/psum | solution.py:221
  274.3 59.4 %all-reduce.23.cloned.1.call-done = (f32[96,1152]{1,0:T(8,128)}, f32[96,384]{1,0:T(8,128)}, f32[96,1536]{1,0:T(8,128)}, f32[384,384]{1,0:T(8,128)}) async-done(((f32[96,1152]{1,0:T(8,128)}, f32[96,384]{1,0:T(8,128)}, f32[96,1536]{1,0:T(8,128)}, f32[384,384]{1,0:T(8,128)}), (f32[96,1152]{1,0:T(8,128)}, f32[96,384]{1,0:T(8,128)}, f32[96,1536]{1,0:T(8,128)}, ...) | async-done | bytes 1769488 | tf_op jit(solution)/shard_map/psum | solution.py:221
  333.7 1.8 copy.110
  335.5 1.6 copy.111
  337.0 1.9 copy.112
  339.0 1.9 copy.113
  (124 shorter events, 8.2 us)
Async XLA Ops:
  7.2 59.8 %all-gather.4.cloned.1.call-start = ((), (), s32[]{:S(2)}) async-start(), calls=%async_computation.4 | async-start | bytes 1474560 | tf_op jit(solution)/shard_map/all_gather | solution.py:77
  7.9 71.1 %all-gather.6.cloned.1.call-start = ((), (), s32[]{:S(2)}) async-start(), calls=%async_computation.5 | async-start | bytes 1474560 | tf_op jit(solution)/shard_map/all_gather | solution.py:79
  8.7 122.8 %reduce-scatter.7.cloned.1.call-start = ((), (), s32[]{:S(2)}) async-start(), calls=%async_computation.7 | async-start | bytes 737280 | tf_op jit(solution)/shard_map/reduce_scatter | solution.py:211
  39.1 2.9 copy-start.17
  46.6 5.3 %copy-start.10 = (bf16[3,197,6,64]{1,3,2,0:T(8,128)(2,1)}, bf16[3,197,6,64]{1,3,2,0:T(8,128)(2,1)S(1)}, u32[]{:S(2)}) copy-start(bf16[3,197,6,64]{1,3,2,0:T(8,128)(2,1)S(1)} %copy.66) | copy-start | bytes 1361668
  51.1 1.5 copy-start.11
  51.8 1.8 copy-start
  52.6 2.0 copy-start.22
  52.6 8.0 %copy-start.23 = (bf16[384]{0:T(512)(128)(2,1)S(1)}, bf16[384]{0:T(512)(128)(2,1)}, u32[]{:S(2)}) copy-start(bf16[384]{0:T(512)(128)(2,1)} %param.28) | copy-start | bytes 2308
  54.6 24.4 %copy-start.15 = (bf16[591,384]{0,1:T(8,128)(2,1)}, bf16[591,384]{0,1:T(8,128)(2,1)S(1)}, u32[]{:S(2)}) copy-start(bf16[591,384]{0,1:T(8,128)(2,1)S(1)} %convert_element_type.126) | copy-start | bytes 1361668
  60.7 18.3 %copy-start.19 = (bf16[384,384]{1,0:T(8,128)(2,1)}, bf16[384,384]{1,0:T(8,128)(2,1)S(1)}, u32[]{:S(2)}) copy-start(bf16[384,384]{1,0:T(8,128)(2,1)S(1)} %all_gather.50) | copy-start | bytes 884740
  66.7 28.4 %copy-start.4 = (f32[591,384]{1,0:T(8,128)}, f32[591,384]{1,0:T(8,128)S(1)}, u32[]{:S(2)}) copy-start(f32[591,384]{1,0:T(8,128)S(1)} %get-tuple-element.69) | copy-start | bytes 2723332
  87.8 7.8 %copy-start.2 = (f32[591,384]{1,0:T(8,128)}, f32[591,384]{1,0:T(8,128)S(1)}, u32[]{:S(2)}) copy-start(f32[591,384]{1,0:T(8,128)S(1)} %reshape.175) | copy-start | bytes 2723332
  87.8 5.9 %copy-start.24 = (bf16[384,1536]{1,0:T(8,128)(2,1)S(1)}, bf16[384,1536]{1,0:T(8,128)(2,1)}, u32[]{:S(2)}) copy-start(bf16[384,1536]{1,0:T(8,128)(2,1)} %all-gather.4.cloned.1.call-done) | copy-start | bytes 3538948
  93.7 1.8 copy-start.25
  95.1 1.5 copy-start.20
  95.1 2.8 copy-start.16
  95.6 1.0 copy-start.6
  102.0 3.4 copy-start.8
  102.0 3.4 copy-start.1
  105.4 1.1 copy-start.12
  107.8 7.2 %copy-start.9 = (bf16[3,197,6,64]{1,3,2,0:T(8,128)(2,1)S(1)}, bf16[3,197,6,64]{1,3,2,0:T(8,128)(2,1)}, u32[]{:S(2)}) copy-start(bf16[3,197,6,64]{1,3,2,0:T(8,128)(2,1)} %copy-done.8) | copy-start | bytes 1361668
  107.8 55.1 %reduce-scatter.5.cloned.1.call-start = ((), (), s32[]{:S(2)}) async-start(), calls=%async_computation.6 | async-start | bytes 2211840 | tf_op jit(solution)/shard_map/reduce_scatter | solution.py:208
  112.7 6.2 %copy-start.13 = (bf16[591,384]{0,1:T(8,128)(2,1)}, bf16[591,384]{0,1:T(8,128)(2,1)S(1)}, u32[]{:S(2)}) copy-start(bf16[591,384]{0,1:T(8,128)(2,1)S(1)} %reshape.177) | copy-start | bytes 1361668
  119.0 3.9 %copy-start.5 = (f32[591,384]{1,0:T(8,128)S(1)}, f32[591,384]{1,0:T(8,128)}, u32[]{:S(2)}) copy-start(f32[591,384]{1,0:T(8,128)} %copy-done.4) | copy-start | bytes 2723332
  119.1 1.2 copy-start.21
  122.8 4.4 %copy-start.3 = (f32[591,384]{1,0:T(8,128)S(1)}, f32[591,384]{1,0:T(8,128)}, u32[]{:S(2)}) copy-start(f32[591,384]{1,0:T(8,128)} %copy-done.2) | copy-start | bytes 2723332
  122.8 75.7 %reduce-scatter.9.cloned.1.call-start = ((), (), s32[]{:S(2)}) async-start(), calls=%async_computation.8 | async-start | bytes 2949120 | tf_op jit(solution)/shard_map/reduce_scatter | solution.py:215
  127.1 106.9 %reduce-scatter.11.cloned.1.call-start = ((), (), s32[]{:S(2)}) async-start(), calls=%async_computation.9 | async-start | bytes 2949120 | tf_op jit(solution)/shard_map/reduce_scatter | solution.py:217
  131.4 103.9 %copy-start.18 = (bf16[384,1152]{1,0:T(8,128)(2,1)S(1)}, bf16[384,1152]{1,0:T(8,128)(2,1)}, u32[]{:S(2)}) copy-start(bf16[384,1152]{1,0:T(8,128)(2,1)} %copy-done.17) | copy-start | bytes 2654212
  131.4 202.2 %all-reduce.23.cloned.1.call-start = ((), (), s32[]{:S(2)}) async-start(), calls=%async_computation.10 | async-start | bytes 3538944 | tf_op jit(solution)/shard_map/psum | solution.py:221
  235.3 3.2 copy-start.7
  238.0 1.7 copy-start.14
Sparse Core Ops, SparseCore 0:
  9.6 20.3 all-gather.3
  31.5 17.4 all-gather.5
  107.9 23.0 reduce-scatter.6
  133.4 29.4 reduce-scatter.4
  165.4 33.0 reduce-scatter.8
  200.9 33.0 reduce-scatter.10
  238.5 95.1 all-reduce.22
where the time goes:
time: 349 us; the launch traced here: 348 us
  waiting for transfers between devices  163 us (47%)
  blocking collectives  62.1 us (18%)
  matrix products  52.7 us (15%)
  local copies, waits for them, and re-layouts  42.1 us (12%)
  between operations  17.4 us (5%)
  other arithmetic  9.41 us (3%)
    psum x1, waiting for transfers between devices, body(): lax.psum((shares[0], shares[1], shares[2], shares[3], shares[4], shares[5...  59.4 us
    reduce_scatter x1, waiting for transfers between devices, body(): lax.psum_scatter(expand_weight_grad, 'shard', scatter_dimension=0, tiled=...  35.6 us
    reduce_scatter x1, waiting for transfers between devices, body(): lax.psum_scatter(reduce_weight_grad, 'shard', scatter_dimension=0, tiled=...  35.5 us
    reduce_scatter x1, waiting for transfers between devices, body(): lax.psum_scatter(project_in_grad, 'shard', scatter_dimension=0, tiled=True)  31.4 us
    psum x1, blocking collectives, body(): lax.psum((shares[0], shares[1], shares[2], shares[3], shares[4], shares[5...  23 us
    unnamed x2, blocking collectives  19.1 us
    unnamed x85, local copies, waits for them, and re-layouts  18.5 us
    dot_general x4, matrix products, outer_sum(): lax.dot_general(left, right, (((0,), (0,)), ((), ())), preferred_element_...  12.2 us
  transfers between devices with their start and end apart: 7, of which 4 were waited for; matrix products, arithmetic and copies ran while one was open for 19% of the time, Pallas kernels for 0%

commit v1 on v0

--- a/solution.py
+++ b/solution.py
@@ -1,6 +1,8 @@
 import jax
 import jax.numpy as jnp
 from jax import lax
+from jax.experimental import pallas as pl
+from jax.experimental.pallas import tpu as pltpu
 from jax.sharding import PartitionSpec as P
 
 HEADS = 6
@@ -256,9 +258,437 @@
     )
 
 
+ROWS = 208
+MESH = pl.DeviceIdType.MESH
+
+
+def mm(left, right):
+    return jnp.dot(left, right, preferred_element_type=jnp.float32)
+
+
+def mega(
+    images_ref, alive_ref, cot_ref, pack_ref, win_ref, wout_ref, wexp_ref, wred_ref,
+    out_ref, ingrad_ref, gin_ref, gout_ref, gexp_ref, gred_ref, gvec_ref,
+    WI, WO, WE, WR, VG, VEC, BE,
+    A1, QKV, PR, MIX, H1, XH1, XH2, RS1, RS2, A2, HID, GP, DM, DU, DH1, DZ, DMX, DT,
+    GB, AR, BS, BR, CS, CR, DR, FIN, ACC, VS, VR,
+    gss, grs, rss, rrs,
+):
+    D = 384
+    slots, length, _ = images_ref.shape
+    replica, shard = lax.axis_index("replica"), lax.axis_index("shard")
+    z, x = replica // 2, replica % 2
+    y, c = shard // 2, shard % 2
+    sib = (replica, y * 2 + 1 - c)
+    ypart = (replica, (1 - y) * 2 + c)
+    xpart = (z * 2 + 1 - x, shard)
+    zparts = [(((z + d) % 4) * 2 + x, shard) for d in (1, 2, 3)]
+
+    barrier = pltpu.get_barrier_semaphore()
+    for who in [sib, ypart, xpart] + zparts:
+        pl.semaphore_signal(barrier, inc=1, device_id=who, device_id_type=MESH)
+    pl.semaphore_wait(barrier, 6)
+
+    def remote(src, dst, ss, rs, who):
+        return pltpu.make_async_remote_copy(
+            src_ref=src, dst_ref=dst, send_sem=ss, recv_sem=rs, device_id=who, device_id_type=MESH
+        )
+
+    items = [(pack_ref, VG, 16), (win_ref, WI, 96), (wout_ref, WO, 96), (wexp_ref, WE, 96), (wred_ref, WR, 384)]
+    other_y = (1 - y) * 2 + c
+    to_y, to_sib, forward = [], [], []
+    for k, (src, full, rows) in enumerate(items):
+        mine = full.at[pl.ds(pl.multiple_of(shard * rows, 16), rows)]
+        theirs = full.at[pl.ds(pl.multiple_of(other_y * rows, 16), rows)]
+        to_y.append(remote(src, mine, gss.at[0, k], grs.at[0, k], ypart))
+        to_sib.append(remote(src, mine, gss.at[1, k], grs.at[1, k], sib))
+        forward.append(remote(theirs, theirs, gss.at[2, k], grs.at[2, k], sib))
+    for k in range(5):
+        to_y[k].start()
+    for k in range(5):
+        to_sib[k].start()
+    for src, full, rows in items:
+        full[pl.ds(pl.multiple_of(shard * rows, 16), rows), :] = src[...]
+
+    def arrived(ks):
+        for k in ks:
+            to_y[k].wait_recv()
+            forward[k].start()
+        for k in ks:
+            to_sib[k].wait_recv()
+            forward[k].wait_recv()
+
+    arrived([0, 1])
+    lane = lax.broadcasted_iota(jnp.int32, (128, D), 1)
+    sub = lax.broadcasted_iota(jnp.int32, (128, D), 0)
+    place = [jnp.where((lane == sub + 96 * s) & (sub < 96), 1.0, 0.0).astype(jnp.bfloat16) for s in range(4)]
+    blocks = [VG[16 * s : 16 * s + 16, :] for s in range(4)]
+    VEC[...] = sum(mm(blocks[s], place[s]) for s in range(4))
+    for s in range(4):
+        BE[s : s + 1, :] = sum(mm(blocks[s], place[k])[8 + k : 9 + k, :] for k in range(4))
+    row = lambda j: VEC[j : j + 1, :]
+    half = lax.broadcasted_iota(jnp.int32, (ROWS, 128), 1) < 64
+    keep = lax.broadcasted_iota(jnp.int32, (ROWS, ROWS), 1) < length
+    scale = HEAD_DIM ** (-0.5)
+    pairs = HEADS // 2
+
+    def at(i):
+        return pl.ds(pl.multiple_of(i * ROWS, 16), ROWS)
+
+    def pad(value):
+        return jnp.concatenate([value, jnp.zeros((ROWS - length, D), value.dtype)], axis=0)
+
+    def norm(value):
+        center = value - jnp.mean(value, -1, keepdims=True)
+        inverse = lax.rsqrt(jnp.mean(center * center, -1, keepdims=True) + EPS)
+        return center * inverse, inverse
+
+    def norm_back(grad, gain, unit, inverse):
+        g = grad * gain
+        return inverse * (g - jnp.mean(g, -1, keepdims=True) - unit * jnp.mean(g * unit, -1, keepdims=True))
+
+    def pick(h, value):
+        zero = jnp.zeros_like(value)
+        return jnp.where(half, value, zero) if h == 0 else jnp.where(half, zero, value)
+
+    def nt(left, right):
+        return lax.dot_general(left, right, (((1,), (1,)), ((), ())), preferred_element_type=jnp.float32)
+
+    def tn(left, right):
+        return lax.dot_general(left, right, (((0,), (0,)), ((), ())), preferred_element_type=jnp.float32)
+
+    @pl.loop(0, slots)
+    def _(i):
+        r = at(i)
+        tokens = pad(images_ref[i].astype(jnp.float32))
+        unit, inverse = norm(tokens)
+        H1[r, :] = tokens
+        XH1[r, :] = unit
+        RS1[r, :] = jnp.broadcast_to(inverse, (ROWS, 128))
+        A1[r, :] = (unit * row(0) + row(1)).astype(jnp.bfloat16)
+        a1 = A1[r, :]
+        QKV[r, 0:D] = (mm(a1, WI[:, 0:D]) + row(2)).astype(jnp.bfloat16)
+        QKV[r, D : 2 * D] = mm(a1, WI[:, D : 2 * D]).astype(jnp.bfloat16)
+        QKV[r, 2 * D : 3 * D] = (mm(a1, WI[:, 2 * D : 3 * D]) + row(3)).astype(jnp.bfloat16)
+        for p in range(pairs):
+            q = QKV[r, p * 128 : p * 128 + 128]
+            k = QKV[r, D + p * 128 : D + p * 128 + 128]
+            v = QKV[r, 2 * D + p * 128 : 2 * D + p * 128 + 128]
+            both = []
+            for h in range(2):
+                scores = jnp.where(keep, nt(pick(h, q), k) * scale, -1e30)
+                e = jnp.exp(scores - jnp.max(scores, -1, keepdims=True))
+                prob = e * (1.0 / jnp.sum(e, -1, keepdims=True))
+                PR[i * HEADS + p * 2 + h] = prob
+                both.append(mm(prob.astype(jnp.bfloat16), v))
+            MIX[r, p * 128 : p * 128 + 128] = jnp.where(half, both[0], both[1]).astype(jnp.bfloat16)
+
+    arrived([2, 3])
+
+    @pl.loop(0, slots)
+    def _(i):
+        r = at(i)
+        middle = H1[r, :] + mm(MIX[r, :], WO[...]) + row(4)
+        H1[r, :] = middle
+        unit, inverse = norm(middle)
+        XH2[r, :] = unit
+        RS2[r, :] = jnp.broadcast_to(inverse, (ROWS, 128))
+        A2[r, :] = (unit * row(5) + row(6)).astype(jnp.bfloat16)
+        a2 = A2[r, :]
+        for s in range(4):
+            cols = slice(s * D, s * D + D)
+            u = mm(a2, WE[:, cols]) + BE[s : s + 1, :]
+            cdf = 0.5 * (1.0 + lax.erf(u * (0.5**0.5)))
+            HID[r, cols] = (u * cdf).astype(jnp.bfloat16)
+            GP[r, cols] = cdf + u * (jnp.exp(-0.5 * u * u) * 0.3989422804014327)
+        DM[r, :] = pad(cot_ref[i].astype(jnp.float32) * alive_ref[i]).astype(jnp.bfloat16)
+
+    arrived([4])
+    VS[...] = jnp.zeros_like(VS)
+
+    def tally(j, value):
+        VS[0, j : j + 1, :] += jnp.sum(value, axis=0, keepdims=True)
+
+    @pl.loop(0, slots)
+    def _(i):
+        r = at(i)
+        result = H1[r, :] + mm(HID[r, :], WR[...]) + row(7)
+        out_ref[i] = (result * alive_ref[i]).astype(jnp.bfloat16)[:length]
+        dm = DM[r, :]
+        tally(7, dm.astype(jnp.float32))
+        for s in range(4):
+            cols = slice(s * D, s * D + D)
+            du = (nt(dm, WR[cols, :]) * GP[r, cols]).astype(jnp.bfloat16)
+            DU[r, cols] = du
+            tally(8 + s, du.astype(jnp.float32))
+
+    def step_a(n):
+        return remote(GB.at[n, 1 - c], AR.at[n], rss.at[n, 0], rrs.at[n, 0], sib)
+
+    def step_b(n):
+        return remote(BS.at[n], BR.at[n], rss.at[n, 1], rrs.at[n, 1], ypart)
+
+    def step_c(n):
+        return remote(CS.at[n, pl.ds(pl.multiple_of((1 - x) * 192, 16), 192)], CR.at[n], rss.at[n, 2], rrs.at[n, 2], xpart)
+
+    def steps_d(n):
+        return [
+            remote(CS.at[n, pl.ds(pl.multiple_of(x * 192 + ((z + d) % 4) * 48, 16), 48)], DR.at[n, d - 1],
+                   rss.at[n, 2 + d], rrs.at[n, 2 + d], zparts[d - 1])
+            for d in (1, 2, 3)
+        ]
+
+    def steps_e(n):
+        piece = FIN.at[n, pl.ds(pl.multiple_of(x * 192 + z * 48, 16), 48)]
+        return [remote(piece, piece, rss.at[n, 5 + d], rrs.at[n, 5 + d], zparts[d - 1]) for d in (1, 2, 3)]
+
+    def step_f(n):
+        piece = FIN.at[n, pl.ds(pl.multiple_of(x * 192, 16), 192)]
+        return remote(piece, piece, rss.at[n, 9], rrs.at[n, 9], xpart)
+
+    def do_a(n):
+        step_a(n).start()
+
+    def do_b(n):
+        step_a(n).wait_recv()
+        BS[n] = (GB[n, c, 1 - y].astype(jnp.float32) + AR[n, 1 - y].astype(jnp.float32)).astype(jnp.bfloat16)
+        step_b(n).start()
+        ACC[n] = GB[n, c, y].astype(jnp.float32) + AR[n, y].astype(jnp.float32)
+
+    def do_c(n):
+        step_b(n).wait_recv()
+        total = ACC[n] + BR[n].astype(jnp.float32)
+        ACC[n] = total
+        CS[n] = total.astype(jnp.bfloat16)
+        step_c(n).start()
+
+    def do_d(n):
+        step_c(n).wait_recv()
+        step_c(n).wait_send()
+        rows = pl.ds(pl.multiple_of(x * 192, 16), 192)
+        total = ACC[n, rows, :] + CR[n].astype(jnp.float32)
+        ACC[n, rows, :] = total
+        CS[n, rows, :] = total.astype(jnp.bfloat16)
+        for copy in steps_d(n):
+            copy.start()
+
+    def do_e(n):
+        for copy in steps_d(n):
+            copy.wait_recv()
+        rows = pl.ds(pl.multiple_of(x * 192 + z * 48, 16), 48)
+        total = ACC[n, rows, :] + DR[n, 0].astype(jnp.float32) + DR[n, 1].astype(jnp.float32) + DR[n, 2].astype(jnp.float32)
+        FIN[n, rows, :] = total.astype(jnp.bfloat16)
+        for copy in steps_e(n):
+            copy.start()
+
+    def do_f(n):
+        for copy in steps_e(n):
+            copy.wait_recv()
+        step_f(n).start()
+
+    def do_end(n):
+        step_f(n).wait_recv()
+
+    def put(n, cols_at, grad):
+        rows = grad.shape[0] // 4
+        for s in range(4):
+            GB[n, s % 2, s // 2, cols_at : cols_at + rows, :] = grad[s * rows : s * rows + rows, :].astype(jnp.bfloat16)
+
+    dm_all = DM[...]
+    for s in range(4):
+        GB[0, s % 2, s // 2] = tn(HID[:, s * D : s * D + D], dm_all).astype(jnp.bfloat16)
+    do_a(0)
+
+    a2_all = A2[...]
+    for s in range(4):
+        put(1, s * 96, tn(a2_all, DU[:, s * D : s * D + D]))
+    do_b(0)
+    do_a(1)
+
+    @pl.loop(0, slots)
+    def _(i):
+        r = at(i)
+        da2 = nt(DU[r, :], WE[...])
+        unit = XH2[r, :]
+        tally(5, da2 * unit)
+        tally(6, da2)
+        dh1 = DM[r, :].astype(jnp.float32) + norm_back(da2, row(5), unit, RS2[r, 0:1])
+        DH1[r, :] = dh1
+        dz = dh1.astype(jnp.bfloat16)
+        DZ[r, :] = dz
+        tally(4, dz.astype(jnp.float32))
+        DMX[r, :] = nt(dz, WO[...]).astype(jnp.bfloat16)
+
+    do_b(1)
+    put(2, 288, tn(MIX[...], DZ[...]))
+
+    def attend_back(i):
+        r = at(i)
+        for p in range(pairs):
+            cols = slice(p * 128, p * 128 + 128)
+            kcols = slice(D + p * 128, D + p * 128 + 128)
+            vcols = slice(2 * D + p * 128, 2 * D + p * 128 + 128)
+            q, k, v, dmx = QKV[r, cols], QKV[r, kcols], QKV[r, vcols], DMX[r, cols]
+            dq, dk, dv = [], 0.0, 0.0
+            for h in range(2):
+                prob = PR[i * HEADS + p * 2 + h]
+                dmh = pick(h, dmx)
+                dv = dv + tn(prob.astype(jnp.bfloat16), dmh)
+                dp = nt(dmh, v)
+                ds = (prob * (dp - jnp.sum(prob * dp, -1, keepdims=True))).astype(jnp.bfloat16)
+                dq.append(mm(ds, k))
+                dk = dk + tn(ds, pick(h, q))
+            dq = (jnp.where(half, dq[0], dq[1]) * scale).astype(jnp.bfloat16)
+            DT[r, cols] = dq
+            DT[r, kcols] = (dk * scale).astype(jnp.bfloat16)
+            DT[r, vcols] = dv.astype(jnp.bfloat16)
+        tally(2, DT[r, 0:D].astype(jnp.float32))
+        tally(3, DT[r, 2 * D : 3 * D].astype(jnp.float32))
+
+    @pl.loop(0, 1)
+    def _(i):
+        attend_back(i)
+
+    do_c(0)
+
+    @pl.loop(1, 2)
+    def _(i):
+        attend_back(i)
+
+    do_d(0)
+    do_c(1)
+
+    @pl.loop(2, slots)
+    def _(i):
+        attend_back(i)
+
+    do_e(0)
+    do_d(1)
+    a1_all = A1[...]
+    for s in range(3):
+        put(2, s * 96, tn(a1_all, DT[:, s * D : s * D + D]))
+    do_a(2)
+    do_f(0)
+    do_e(1)
+
+    @pl.loop(0, slots)
+    def _(i):
+        r = at(i)
+        da1 = nt(DT[r, :], WI[...])
+        unit = XH1[r, :]
+        tally(0, da1 * unit)
+        tally(1, da1)
+        grad = DH1[r, :] + norm_back(da1, row(0), unit, RS1[r, 0:1])
+        ingrad_ref[i] = grad.astype(jnp.bfloat16)[:length]
+
+    zone = ((z + 1 - 2 * (z % 2)) * 2 + x, shard)
+    vec_steps = [
+        remote(VS.at[k], VR.at[k], rss.at[3, k], rrs.at[3, k], who)
+        for k, who in enumerate([sib, ypart, xpart, zone, zparts[1]])
+    ]
+
+    def vec(k):
+        if k > 0:
+            vec_steps[k - 1].wait_recv()
+            VS[k] = VS[k - 1] + VR[k - 1]
+        if k < 5:
+            vec_steps[k].start()
+
+    do_b(2)
+    vec(0)
+    do_f(1)
+    do_end(0)
+    gred_ref[...] = FIN[0].astype(jnp.float32)
+    vec(1)
+    do_c(2)
+    vec(2)
+    do_d(2)
+    vec(3)
+    do_end(1)
+    for s in range(4):
+        gexp_ref[:, s * D : s * D + D] = FIN[1, s * 96 : s * 96 + 96, :].astype(jnp.float32)
+    do_e(2)
+    vec(4)
+    do_f(2)
+    vec(5)
+    gvec_ref[...] = VS[5]
+    do_end(2)
+    for s in range(3):
+        gin_ref[:, s * D : s * D + D] = FIN[2, s * 96 : s * 96 + 96, :].astype(jnp.float32)
+    gout_ref[...] = FIN[2, 288:384, :].astype(jnp.float32)
+
+    for k in range(5):
+        to_y[k].wait_send()
+        to_sib[k].wait_send()
+        forward[k].wait_send()
+        vec_steps[k].wait_send()
+    for n in range(3):
+        step_a(n).wait_send()
+        step_b(n).wait_send()
+        for copy in steps_d(n) + steps_e(n):
+            copy.wait_send()
+        step_f(n).wait_send()
+
+
+def fused_body(
+    images, counts, first_gain, first_shift, project_in, query_bias, value_bias, project_out, output_bias,
+    second_gain, second_shift, expand_weight, expand_bias, reduce_weight, reduce_bias, cotangent,
+):
+    slots, length, width = images.shape
+    alive = (jnp.arange(slots) < counts[0]).astype(jnp.float32)
+    rows = [first_gain, first_shift, query_bias, value_bias, output_bias, second_gain, second_shift, reduce_bias]
+    pack = jnp.concatenate([jnp.stack(rows), expand_bias.reshape(4, 96)], axis=0)
+    pack = jnp.pad(pack, ((0, 4), (0, 32)))
+    f32, b16 = jnp.float32, jnp.bfloat16
+    n = slots * ROWS
+    vm = pl.BlockSpec(memory_space=pltpu.VMEM)
+    scratch = [
+        ((384, 1152), b16), ((384, 384), b16), ((384, 1536), b16), ((1536, 384), b16), ((64, 128), b16),
+        ((16, 384), f32), ((8, 384), f32),
+        ((n, 384), b16), ((n, 1152), b16), ((slots * HEADS, ROWS, ROWS), f32), ((n, 384), b16), ((n, 384), f32),
+        ((n, 384), f32), ((n, 384), f32), ((n, 128), f32), ((n, 128), f32), ((n, 384), b16), ((n, 1536), b16),
+        ((n, 1536), f32), ((n, 384), b16), ((n, 1536), b16), ((n, 384), f32), ((n, 384), b16), ((n, 384), b16),
+        ((n, 1152), b16),
+        ((3, 2, 2, 384, 384), b16), ((3, 2, 384, 384), b16), ((3, 384, 384), b16), ((3, 384, 384), b16),
+        ((3, 384, 384), b16), ((3, 192, 384), b16), ((3, 3, 48, 384), b16), ((3, 384, 384), b16), ((3, 384, 384), f32),
+        ((6, 16, 384), f32), ((5, 16, 384), f32),
+    ]
+    outs = pl.pallas_call(
+        mega,
+        out_shape=[
+            jax.ShapeDtypeStruct(images.shape, b16),
+            jax.ShapeDtypeStruct(images.shape, b16),
+            jax.ShapeDtypeStruct((96, 1152), f32),
+            jax.ShapeDtypeStruct((96, 384), f32),
+            jax.ShapeDtypeStruct((96, 1536), f32),
+            jax.ShapeDtypeStruct((384, 384), f32),
+            jax.ShapeDtypeStruct((16, 384), f32),
+        ],
+        in_specs=[vm, pl.BlockSpec(memory_space=pltpu.SMEM)] + [vm] * 6,
+        out_specs=[vm] * 7,
+        scratch_shapes=[pltpu.VMEM(shape, kind) for shape, kind in scratch]
+        + [
+            pltpu.SemaphoreType.DMA((3, 5)),
+            pltpu.SemaphoreType.DMA((3, 5)),
+            pltpu.SemaphoreType.DMA((4, 10)),
+            pltpu.SemaphoreType.DMA((4, 10)),
+        ],
+        compiler_params=pltpu.CompilerParams(collective_id=0, has_side_effects=True, vmem_limit_bytes=60 * 2**20),
+    )(images, alive, cotangent, pack, project_in, project_out, expand_weight, reduce_weight)
+    out, ingrad, gin, gout, gexp, gred, gvec = outs
+    shard = lax.axis_index("shard")
+    part = lax.dynamic_slice(gvec, (0, shard * 96), (8, 96))
+    gbe = lax.dynamic_slice(gvec, (8 + shard, 0), (1, 384))[0]
+    return (
+        out, ingrad, part[0], part[1], gin, part[2], part[3], gout, part[4], part[5], part[6],
+        gexp, gbe, gred, part[7],
+    )
+
+
 def solution(mesh):
+    fits = mesh.shape["replica"] == 8 and mesh.shape["shard"] == 4
     return jax.shard_map(
-        body,
+        fused_body if fits else body,
         mesh=mesh,
         in_specs=(
             P(("replica", "shard"), None, None),

time: 349 us -> 104 us (0.30)
  waiting for transfers between devices: 163 us -> 0 us
  Pallas kernels: 0 us -> 90.5 us
  blocking collectives: 62.1 us -> 0 us
  matrix products: 52.7 us -> 0 us
  local copies, waits for them, and re-layouts: 42.1 us -> 11.5 us
  between operations: 17.4 us -> 1.35 us
  other arithmetic: 9.41 us -> 0.51 us
    reduce_scatter x4 -> x0, waiting for transfers between devices: 103 us -> none  [the longest x1 35.6 us: body(): lax.psum_scatter(expand_weight_grad, 'shard', scatter_dimension=0, tiled=...]
    pallas_call x0 -> x1, Pallas kernels: none -> 90.5 us  [fused_body(): pl.pallas_call(mega, out_shape=[jax.ShapeDtypeStruct(images.shape, b16),...]
    psum x1 -> x0, waiting for transfers between devices: 59.4 us -> none  [body(): lax.psum((shares[0], shares[1], shares[2], shares[3], shares[4], shares[5...]
    dot_general x18 -> x0, matrix products: 52.7 us -> none  [the longest x4 12.2 us: outer_sum(): lax.dot_general(left, right, (((0,), (0,)), ((), ())), preferred_element_...]
    psum x1 -> x0, blocking collectives: 23 us -> none  [body(): lax.psum((shares[0], shares[1], shares[2], shares[3], shares[4], shares[5...]
    all_gather x3 -> x0, blocking collectives: 20 us -> none  [the longest x1 8.64 us: body(): lax.all_gather(project_in, 'shard', axis=0, tiled=True)]
    unnamed x2 -> x0, blocking collectives: 19.1 us -> none
    reshape x14 -> x1, local copies, waits for them, and re-layouts: 16.9 us -> 0.09 us  [fused_body(): expand_bias.reshape(4, 96)]
  transfers between devices with their start and end apart: 7 -> 0, of which waited for: 4 -> 0; matrix products, arithmetic and copies ran while one was open for 19% -> 0% of each run, Pallas kernels for 0% -> 0%
where the time goes in v1:
time: 104 us
  Pallas kernels  90.5 us (87%)
  local copies, waits for them, and re-layouts  11.5 us (11%)
  between operations  1.35 us (1%)
    pallas_call x1, Pallas kernels, fused_body(): pl.pallas_call(mega, out_shape=[jax.ShapeDtypeStruct(images.shape, b16),...  90.5 us
    unnamed x34, local copies, waits for them, and re-layouts  8.16 us

profile of v1, /device:TPU:0, one launch (start us, length us, event | category | flops | bytes accessed | tf_op | source)
XLA Modules:
  0.0 103.9 jit_solution(8932912460958829089)
XLA Ops:
  1.3 0.5 compare_convert_fusion.alive_ref
  1.8 0.0 copy-start.11
  1.8 0.0 copy-start.12
  1.8 0.0 copy-start.13
  1.8 0.0 copy-start.5
  1.8 0.0 copy-start.10
  1.8 0.7 copy-done.5
  2.5 0.0 copy-start.6
  2.5 0.0 copy-start.7
  2.5 0.0 copy-start.8
  2.5 0.0 copy-start.9
  2.5 0.1 reshape.33
  2.6 0.0 copy-done.11
  2.6 0.0 copy-done.12
  2.6 0.0 copy-done.13
  2.6 0.0 copy-done.10
  2.7 0.5 copy-done.6
  3.2 0.0 copy-done.7
  3.2 0.0 copy-done.8
  3.2 0.0 copy-done.9
  3.2 0.1 concatenate.3
  3.3 0.6 pad.4.pack_ref
  3.9 90.5 %shard_map.271 = (bf16[3,197,384]{2,1,0:T(8,128)(2,1)}, bf16[3,197,384]{2,1,0:T(8,128)(2,1)}, f32[96,1152]{1,0:T(8,128)}, f32[96,384]{1,0:T(8,128)}, f32[96,1536...) custom-call(bf16[3,197,384]{2,1,0:T(8,128)(2,1)} %images_ref.1, f32[3]{0:T(128)} %compare_convert_fusion.alive_ref, ...), custom_call_target="tpu_custom_call" | custom-call | tf_op jit(solution)/shard_map/pallas_call | solution.py:656
  94.4 1.3 %dynamic-slice_reduce_fusion = f32[384]{0:T(512)} fusion(f32[16,384]{1,0:T(8,128)} %get-tuple-element.24, s32[]{:T(128)S(6)} %select_n.7), kind=kLoop, calls=%fused_computation.1 | loop fusion | bytes 3076 | tf_op jit(solution)/shard_map/dynamic_slice | solution.py:681
  95.7 0.8 constant_dynamic-slice_fusion
  96.5 0.5 slice_bitcast_fusion
  97.0 0.0 copy-start.2
  97.0 1.9 %copy.38 = bf16[3,197,384]{2,1,0:T(8,128)(2,1)} copy(bf16[3,197,384]{2,1,0:T(8,128)(2,1)} %get-tuple-element.52) | data formatting | bytes 907776
  98.9 0.0 copy-done.2
  98.9 0.0 copy-start.3
  98.9 0.8 copy.39
  99.7 0.4 copy-done.3
  100.1 0.0 copy-start.4
  100.1 0.0 copy-start.1
  100.1 0.8 copy.40
  100.9 0.3 copy-done.4
  101.1 0.7 copy.41
  101.8 0.0 copy-done.1
  101.8 0.0 copy-start
  101.8 0.8 copy.42
  102.6 0.5 copy-done
  103.1 0.8 copy.43
Async XLA Ops:
  1.8 0.8 copy-start.11
  1.8 0.8 copy-start.12
  1.8 0.8 copy-start.13
  1.8 0.7 copy-start.5
  1.8 0.8 copy-start.10
  2.5 0.7 copy-start.6
  2.5 0.7 copy-start.7
  2.5 0.7 copy-start.8
  2.5 0.7 copy-start.9
  97.0 1.9 %copy-start.2 = (bf16[3,197,384]{2,1,0:T(8,128)(2,1)S(1)}, bf16[3,197,384]{2,1,0:T(8,128)(2,1)}, u32[]{:S(2)}) copy-start(bf16[3,197,384]{2,1,0:T(8,128)(2,1)} %get-tuple-element.53) | copy-start | bytes 1361668
  98.9 1.2 %copy-start.3 = (f32[96,1152]{1,0:T(8,128)S(1)}, f32[96,1152]{1,0:T(8,128)}, u32[]{:S(2)}) copy-start(f32[96,1152]{1,0:T(8,128)} %get-tuple-element.56) | copy-start | bytes 1327108
  100.1 1.0 copy-start.4
  100.1 1.7 %copy-start.1 = (f32[96,1536]{1,0:T(8,128)S(1)}, f32[96,1536]{1,0:T(8,128)}, u32[]{:S(2)}) copy-start(f32[96,1536]{1,0:T(8,128)} %get-tuple-element.63) | copy-start | bytes 1769476
  101.8 1.3 %copy-start = (f32[384,384]{1,0:T(8,128)S(1)}, f32[384,384]{1,0:T(8,128)}, u32[]{:S(2)}) copy-start(f32[384,384]{1,0:T(8,128)} %get-tuple-element.65) | copy-start | bytes 1769476

commit v2 on v1

--- a/solution.py
+++ b/solution.py
@@ -267,12 +267,12 @@
 
 
 def mega(
-    images_ref, alive_ref, cot_ref, pack_ref, win_ref, wout_ref, wexp_ref, wred_ref,
-    out_ref, ingrad_ref, gin_ref, gout_ref, gexp_ref, gred_ref, gvec_ref,
+    images_ref, counts_ref, cot_ref, pack_ref, win_ref, wout_ref, wexp_ref, wred_ref,
+    out_ref, ingrad_ref, FIN, gvec_ref,
     WI, WO, WE, WR, VG, VEC, BE,
     A1, QKV, PR, MIX, H1, XH1, XH2, RS1, RS2, A2, HID, GP, DM, DU, DH1, DZ, DMX, DT,
-    GB, AR, BS, BR, CS, CR, DR, FIN, ACC, VS, VR,
-    gss, grs, rss, rrs,
+    GB, AR, BS, BR, CS, CR, DR, ACC, V0, V1, V2,
+    gss, grs, rss, rrs, vss, vrs,
 ):
     D = 384
     slots, length, _ = images_ref.shape
@@ -285,9 +285,11 @@
     zparts = [(((z + d) % 4) * 2 + x, shard) for d in (1, 2, 3)]
 
     barrier = pltpu.get_barrier_semaphore()
-    for who in [sib, ypart, xpart] + zparts:
+    group = [(replica, (shard + d) % 4) for d in (1, 2, 3)]
+    replicas = [((replica + d) % 8, shard) for d in range(1, 8)]
+    for who in group + replicas:
         pl.semaphore_signal(barrier, inc=1, device_id=who, device_id_type=MESH)
-    pl.semaphore_wait(barrier, 6)
+    pl.semaphore_wait(barrier, 10)
 
     def remote(src, dst, ss, rs, who):
         return pltpu.make_async_remote_copy(
@@ -296,13 +298,20 @@
 
     items = [(pack_ref, VG, 16), (win_ref, WI, 96), (wout_ref, WO, 96), (wexp_ref, WE, 96), (wred_ref, WR, 384)]
     other_y = (1 - y) * 2 + c
-    to_y, to_sib, forward = [], [], []
+    to_y, to_sib, near, to_x, far = [], [], [], [], []
     for k, (src, full, rows) in enumerate(items):
+        part = rows // 2 if k else rows
+        near_at = x * part if k else 0
+        far_at = (1 - x) * part if k else 0
         mine = full.at[pl.ds(pl.multiple_of(shard * rows, 16), rows)]
-        theirs = full.at[pl.ds(pl.multiple_of(other_y * rows, 16), rows)]
-        to_y.append(remote(src, mine, gss.at[0, k], grs.at[0, k], ypart))
+        sent = full.at[pl.ds(pl.multiple_of(shard * rows + near_at, 16), part)]
+        got = full.at[pl.ds(pl.multiple_of(other_y * rows + near_at, 16), part)]
+        rest = full.at[pl.ds(pl.multiple_of(other_y * rows + far_at, 16), part)]
+        to_y.append(remote(src.at[pl.ds(pl.multiple_of(near_at, 16), part)] if k else src, sent, gss.at[0, k], grs.at[0, k], ypart))
         to_sib.append(remote(src, mine, gss.at[1, k], grs.at[1, k], sib))
-        forward.append(remote(theirs, theirs, gss.at[2, k], grs.at[2, k], sib))
+        near.append(remote(got, got, gss.at[2, k], grs.at[2, k], sib))
+        to_x.append(remote(got, got, gss.at[3, k], grs.at[3, k], xpart))
+        far.append(remote(rest, rest, gss.at[4, k], grs.at[4, k], sib))
     for k in range(5):
         to_y[k].start()
     for k in range(5):
@@ -310,15 +319,26 @@
     for src, full, rows in items:
         full[pl.ds(pl.multiple_of(shard * rows, 16), rows), :] = src[...]
 
-    def arrived(ks):
-        for k in ks:
-            to_y[k].wait_recv()
-            forward[k].start()
-        for k in ks:
-            to_sib[k].wait_recv()
-            forward[k].wait_recv()
-
-    arrived([0, 1])
+    def relay_y(k):
+        to_y[k].wait_recv()
+        if k:
+            to_x[k].start()
+        near[k].start()
+
+    def relay_x(k):
+        if k:
+            to_x[k].wait_recv()
+            far[k].start()
+
+    def settle(k):
+        to_sib[k].wait_recv()
+        near[k].wait_recv()
+        if k:
+            far[k].wait_recv()
+
+    for relay in (relay_y, relay_x, settle):
+        for k in (0, 1):
+            relay(k)
     lane = lax.broadcasted_iota(jnp.int32, (128, D), 1)
     sub = lax.broadcasted_iota(jnp.int32, (128, D), 0)
     place = [jnp.where((lane == sub + 96 * s) & (sub < 96), 1.0, 0.0).astype(jnp.bfloat16) for s in range(4)]
@@ -332,6 +352,9 @@
     scale = HEAD_DIM ** (-0.5)
     pairs = HEADS // 2
 
+    def alive(i):
+        return jnp.where(i < counts_ref[0], 1.0, 0.0).astype(jnp.float32)
+
     def at(i):
         return pl.ds(pl.multiple_of(i * ROWS, 16), ROWS)
 
@@ -360,6 +383,17 @@
     @pl.loop(0, slots)
     def _(i):
         r = at(i)
+
+        @pl.when(i == 1)
+        def _():
+            relay_y(2)
+            relay_y(3)
+
+        @pl.when(i == 2)
+        def _():
+            relay_x(2)
+            relay_x(3)
+
         tokens = pad(images_ref[i].astype(jnp.float32))
         unit, inverse = norm(tokens)
         H1[r, :] = tokens
@@ -383,11 +417,18 @@
                 both.append(mm(prob.astype(jnp.bfloat16), v))
             MIX[r, p * 128 : p * 128 + 128] = jnp.where(half, both[0], both[1]).astype(jnp.bfloat16)
 
-    arrived([2, 3])
+    settle(2)
+    relay_y(4)
+    settle(3)
 
     @pl.loop(0, slots)
     def _(i):
         r = at(i)
+
+        @pl.when(i == 1)
+        def _():
+            relay_x(4)
+
         middle = H1[r, :] + mm(MIX[r, :], WO[...]) + row(4)
         H1[r, :] = middle
         unit, inverse = norm(middle)
@@ -401,19 +442,19 @@
             cdf = 0.5 * (1.0 + lax.erf(u * (0.5**0.5)))
             HID[r, cols] = (u * cdf).astype(jnp.bfloat16)
             GP[r, cols] = cdf + u * (jnp.exp(-0.5 * u * u) * 0.3989422804014327)
-        DM[r, :] = pad(cot_ref[i].astype(jnp.float32) * alive_ref[i]).astype(jnp.bfloat16)
-
-    arrived([4])
-    VS[...] = jnp.zeros_like(VS)
+        DM[r, :] = pad(cot_ref[i].astype(jnp.float32) * alive(i)).astype(jnp.bfloat16)
+
+    settle(4)
+    V0[...] = jnp.zeros_like(V0)
 
     def tally(j, value):
-        VS[0, j : j + 1, :] += jnp.sum(value, axis=0, keepdims=True)
+        V0[j : j + 1, :] += jnp.sum(value, axis=0, keepdims=True)
 
     @pl.loop(0, slots)
     def _(i):
         r = at(i)
         result = H1[r, :] + mm(HID[r, :], WR[...]) + row(7)
-        out_ref[i] = (result * alive_ref[i]).astype(jnp.bfloat16)[:length]
+        out_ref[i] = (result * alive(i)).astype(jnp.bfloat16)[:length]
         dm = DM[r, :]
         tally(7, dm.astype(jnp.float32))
         for s in range(4):
@@ -422,62 +463,86 @@
             DU[r, cols] = du
             tally(8 + s, du.astype(jnp.float32))
 
+    chunks = [(m, off, size) for m in range(3) for off, size in ((0, 256), (256, 128))]
+
+    def span(n, at_row, size):
+        return pl.ds(pl.multiple_of(chunks[n][1] + at_row, 16), size)
+
     def step_a(n):
-        return remote(GB.at[n, 1 - c], AR.at[n], rss.at[n, 0], rrs.at[n, 0], sib)
+        m, off, size = chunks[n]
+        rows = pl.ds(off, size)
+        return remote(GB.at[m, 1 - c, :, rows], AR.at[m, :, rows], rss.at[n, 0], rrs.at[n, 0], sib)
 
     def step_b(n):
-        return remote(BS.at[n], BR.at[n], rss.at[n, 1], rrs.at[n, 1], ypart)
+        m, off, size = chunks[n]
+        rows = pl.ds(off, size)
+        return remote(BS.at[m, rows], BR.at[m, rows], rss.at[n, 1], rrs.at[n, 1], ypart)
 
     def step_c(n):
-        return remote(CS.at[n, pl.ds(pl.multiple_of((1 - x) * 192, 16), 192)], CR.at[n], rss.at[n, 2], rrs.at[n, 2], xpart)
+        m, off, size = chunks[n]
+        src = CS.at[m, span(n, (1 - x) * (size // 2), size // 2)]
+        return remote(src, CR.at[m, pl.ds(off // 2, size // 2)], rss.at[n, 2], rrs.at[n, 2], xpart)
 
     def steps_d(n):
+        m, off, size = chunks[n]
         return [
-            remote(CS.at[n, pl.ds(pl.multiple_of(x * 192 + ((z + d) % 4) * 48, 16), 48)], DR.at[n, d - 1],
+            remote(CS.at[m, span(n, x * (size // 2) + ((z + d) % 4) * (size // 8), size // 8)],
+                   DR.at[m, d - 1, pl.ds(off // 8, size // 8)],
                    rss.at[n, 2 + d], rrs.at[n, 2 + d], zparts[d - 1])
             for d in (1, 2, 3)
         ]
 
     def steps_e(n):
-        piece = FIN.at[n, pl.ds(pl.multiple_of(x * 192 + z * 48, 16), 48)]
+        m, off, size = chunks[n]
+        piece = FIN.at[m, span(n, x * (size // 2) + z * (size // 8), size // 8)]
         return [remote(piece, piece, rss.at[n, 5 + d], rrs.at[n, 5 + d], zparts[d - 1]) for d in (1, 2, 3)]
 
     def step_f(n):
-        piece = FIN.at[n, pl.ds(pl.multiple_of(x * 192, 16), 192)]
+        m, off, size = chunks[n]
+        piece = FIN.at[m, span(n, x * (size // 2), size // 2)]
         return remote(piece, piece, rss.at[n, 9], rrs.at[n, 9], xpart)
 
     def do_a(n):
         step_a(n).start()
 
     def do_b(n):
+        m, off, size = chunks[n]
+        rows = slice(off, off + size)
         step_a(n).wait_recv()
-        BS[n] = (GB[n, c, 1 - y].astype(jnp.float32) + AR[n, 1 - y].astype(jnp.float32)).astype(jnp.bfloat16)
+        BS[m, rows, :] = (
+            GB[m, c, 1 - y, rows, :].astype(jnp.float32) + AR[m, 1 - y, rows, :].astype(jnp.float32)
+        ).astype(jnp.bfloat16)
         step_b(n).start()
-        ACC[n] = GB[n, c, y].astype(jnp.float32) + AR[n, y].astype(jnp.float32)
+        ACC[m, rows, :] = GB[m, c, y, rows, :].astype(jnp.float32) + AR[m, y, rows, :].astype(jnp.float32)
 
     def do_c(n):
+        m, off, size = chunks[n]
+        rows = slice(off, off + size)
         step_b(n).wait_recv()
-        total = ACC[n] + BR[n].astype(jnp.float32)
-        ACC[n] = total
-        CS[n] = total.astype(jnp.bfloat16)
+        total = ACC[m, rows, :] + BR[m, rows, :].astype(jnp.float32)
+        ACC[m, rows, :] = total
+        CS[m, rows, :] = total.astype(jnp.bfloat16)
         step_c(n).start()
 
     def do_d(n):
+        m, off, size = chunks[n]
         step_c(n).wait_recv()
-        step_c(n).wait_send()
-        rows = pl.ds(pl.multiple_of(x * 192, 16), 192)
-        total = ACC[n, rows, :] + CR[n].astype(jnp.float32)
-        ACC[n, rows, :] = total
-        CS[n, rows, :] = total.astype(jnp.bfloat16)
+        rows = span(n, x * (size // 2), size // 2)
+        total = ACC[m, rows, :] + CR[m, off // 2 : off // 2 + size // 2, :].astype(jnp.float32)
+        ACC[m, rows, :] = total
+        CS[m, rows, :] = total.astype(jnp.bfloat16)
         for copy in steps_d(n):
             copy.start()
 
     def do_e(n):
+        m, off, size = chunks[n]
         for copy in steps_d(n):
             copy.wait_recv()
-        rows = pl.ds(pl.multiple_of(x * 192 + z * 48, 16), 48)
-        total = ACC[n, rows, :] + DR[n, 0].astype(jnp.float32) + DR[n, 1].astype(jnp.float32) + DR[n, 2].astype(jnp.float32)
-        FIN[n, rows, :] = total.astype(jnp.bfloat16)
+        rows = span(n, x * (size // 2) + z * (size // 8), size // 8)
+        total = ACC[m, rows, :]
+        for d in range(3):
+            total = total + DR[m, d, off // 8 : off // 8 + size // 8, :].astype(jnp.float32)
+        FIN[m, rows, :] = total.astype(jnp.bfloat16)
         for copy in steps_e(n):
             copy.start()
 
@@ -489,6 +554,14 @@
     def do_end(n):
         step_f(n).wait_recv()
 
+    stages = [do_a, do_b, do_c, do_d, do_e, do_f, do_end]
+    starts = [0, 1, 2, 3, 7, 8]
+
+    def slot(t):
+        for n in range(6):
+            if 0 <= t - starts[n] < 7:
+                stages[t - starts[n]](n)
+
     def put(n, cols_at, grad):
         rows = grad.shape[0] // 4
         for s in range(4):
@@ -497,13 +570,14 @@
     dm_all = DM[...]
     for s in range(4):
         GB[0, s % 2, s // 2] = tn(HID[:, s * D : s * D + D], dm_all).astype(jnp.bfloat16)
-    do_a(0)
+    slot(0)
+    slot(1)
 
     a2_all = A2[...]
     for s in range(4):
         put(1, s * 96, tn(a2_all, DU[:, s * D : s * D + D]))
-    do_b(0)
-    do_a(1)
+    slot(2)
+    slot(3)
 
     @pl.loop(0, slots)
     def _(i):
@@ -519,10 +593,19 @@
         tally(4, dz.astype(jnp.float32))
         DMX[r, :] = nt(dz, WO[...]).astype(jnp.bfloat16)
 
-    do_b(1)
+    slot(4)
     put(2, 288, tn(MIX[...], DZ[...]))
 
-    def attend_back(i):
+    @pl.loop(0, slots)
+    def _(i):
+        @pl.when(i == 1)
+        def _():
+            slot(5)
+
+        @pl.when(i == 2)
+        def _():
+            slot(6)
+
         r = at(i)
         for p in range(pairs):
             cols = slice(p * 128, p * 128 + 128)
@@ -545,35 +628,24 @@
         tally(2, DT[r, 0:D].astype(jnp.float32))
         tally(3, DT[r, 2 * D : 3 * D].astype(jnp.float32))
 
-    @pl.loop(0, 1)
-    def _(i):
-        attend_back(i)
-
-    do_c(0)
-
-    @pl.loop(1, 2)
-    def _(i):
-        attend_back(i)
-
-    do_d(0)
-    do_c(1)
-
-    @pl.loop(2, slots)
-    def _(i):
-        attend_back(i)
-
-    do_e(0)
-    do_d(1)
     a1_all = A1[...]
     for s in range(3):
         put(2, s * 96, tn(a1_all, DT[:, s * D : s * D + D]))
-    do_a(2)
-    do_f(0)
-    do_e(1)
+    slot(7)
+    slot(8)
 
     @pl.loop(0, slots)
     def _(i):
         r = at(i)
+
+        @pl.when(i == 1)
+        def _():
+            slot(9)
+
+        @pl.when(i == 2)
+        def _():
+            slot(10)
+
         da1 = nt(DT[r, :], WI[...])
         unit = XH1[r, :]
         tally(0, da1 * unit)
@@ -581,53 +653,74 @@
         grad = DH1[r, :] + norm_back(da1, row(0), unit, RS1[r, 0:1])
         ingrad_ref[i] = grad.astype(jnp.bfloat16)[:length]
 
-    zone = ((z + 1 - 2 * (z % 2)) * 2 + x, shard)
-    vec_steps = [
-        remote(VS.at[k], VR.at[k], rss.at[3, k], rrs.at[3, k], who)
-        for k, who in enumerate([sib, ypart, xpart, zone, zparts[1]])
+    group_sends = [
+        remote(V0, V1.at[shard], vss.at[d], vrs.at[d], who) for d, who in enumerate(group)
     ]
-
-    def vec(k):
-        if k > 0:
-            vec_steps[k - 1].wait_recv()
-            VS[k] = VS[k - 1] + VR[k - 1]
-        if k < 5:
-            vec_steps[k].start()
-
-    do_b(2)
-    vec(0)
-    do_f(1)
-    do_end(0)
-    gred_ref[...] = FIN[0].astype(jnp.float32)
-    vec(1)
-    do_c(2)
-    vec(2)
-    do_d(2)
-    vec(3)
-    do_end(1)
-    for s in range(4):
-        gexp_ref[:, s * D : s * D + D] = FIN[1, s * 96 : s * 96 + 96, :].astype(jnp.float32)
-    do_e(2)
-    vec(4)
-    do_f(2)
-    vec(5)
-    gvec_ref[...] = VS[5]
-    do_end(2)
-    for s in range(3):
-        gin_ref[:, s * D : s * D + D] = FIN[2, s * 96 : s * 96 + 96, :].astype(jnp.float32)
-    gout_ref[...] = FIN[2, 288:384, :].astype(jnp.float32)
+    for copy in group_sends:
+        copy.start()
+    V1[shard] = V0[...]
+    slot(11)
+    for copy in group_sends:
+        copy.wait_recv()
+    V2[replica] = V1[0] + V1[1] + V1[2] + V1[3]
+    replica_sends = [
+        remote(V2.at[replica], V2.at[replica], vss.at[3 + d], vrs.at[3 + d], who) for d, who in enumerate(replicas)
+    ]
+    for copy in replica_sends:
+        copy.start()
+    slot(12)
+    slot(13)
+    for copy in replica_sends:
+        copy.wait_recv()
+    gvec_ref[...] = sum([V2[k] for k in range(1, 8)], V2[0])
+    slot(14)
 
     for k in range(5):
         to_y[k].wait_send()
         to_sib[k].wait_send()
-        forward[k].wait_send()
-        vec_steps[k].wait_send()
-    for n in range(3):
+        near[k].wait_send()
+        if k:
+            to_x[k].wait_send()
+            far[k].wait_send()
+    for copy in group_sends + replica_sends:
+        copy.wait_send()
+    for n in range(6):
         step_a(n).wait_send()
         step_b(n).wait_send()
+        step_c(n).wait_send()
         for copy in steps_d(n) + steps_e(n):
             copy.wait_send()
         step_f(n).wait_send()
+
+
+def finish(
+    out_in, ingrad_in, sums, vectors, out_ref, ingrad_ref, gin_ref, gout_ref, gexp_ref, gred_ref, gbe_ref, *rest
+):
+    D = 384
+    vector_refs, sem = rest[:8], rest[8]
+    copies = [
+        pltpu.make_async_copy(out_in, out_ref, sem.at[0]),
+        pltpu.make_async_copy(ingrad_in, ingrad_ref, sem.at[1]),
+    ]
+    for copy in copies:
+        copy.start()
+    shard = lax.axis_index("shard")
+    mine, expand = jnp.zeros((8, 96), jnp.float32), jnp.zeros((1, D), jnp.float32)
+    for s in range(4):
+        chosen = jnp.where(shard == s, 1.0, 0.0).astype(jnp.float32)
+        mine = mine + chosen * vectors[0:8, s * 96 : s * 96 + 96]
+        expand = expand + chosen * vectors[8 + s : 9 + s, :]
+    for j in range(8):
+        vector_refs[j][...] = mine[j : j + 1, :]
+    gbe_ref[...] = expand
+    gred_ref[...] = sums[0].astype(jnp.float32)
+    for s in range(4):
+        gexp_ref[:, s * D : s * D + D] = sums[1, s * 96 : s * 96 + 96, :].astype(jnp.float32)
+    for s in range(3):
+        gin_ref[:, s * D : s * D + D] = sums[2, s * 96 : s * 96 + 96, :].astype(jnp.float32)
+    gout_ref[...] = sums[2, 288:384, :].astype(jnp.float32)
+    for copy in copies:
+        copy.wait()
 
 
 def fused_body(
@@ -635,7 +728,6 @@
     second_gain, second_shift, expand_weight, expand_bias, reduce_weight, reduce_bias, cotangent,
 ):
     slots, length, width = images.shape
-    alive = (jnp.arange(slots) < counts[0]).astype(jnp.float32)
     rows = [first_gain, first_shift, query_bias, value_bias, output_bias, second_gain, second_shift, reduce_bias]
     pack = jnp.concatenate([jnp.stack(rows), expand_bias.reshape(4, 96)], axis=0)
     pack = jnp.pad(pack, ((0, 4), (0, 32)))
@@ -650,11 +742,34 @@
         ((n, 1536), f32), ((n, 384), b16), ((n, 1536), b16), ((n, 384), f32), ((n, 384), b16), ((n, 384), b16),
         ((n, 1152), b16),
         ((3, 2, 2, 384, 384), b16), ((3, 2, 384, 384), b16), ((3, 384, 384), b16), ((3, 384, 384), b16),
-        ((3, 384, 384), b16), ((3, 192, 384), b16), ((3, 3, 48, 384), b16), ((3, 384, 384), b16), ((3, 384, 384), f32),
-        ((6, 16, 384), f32), ((5, 16, 384), f32),
+        ((3, 384, 384), b16), ((3, 192, 384), b16), ((3, 3, 48, 384), b16), ((3, 384, 384), f32),
+        ((16, 384), f32), ((4, 16, 384), f32), ((8, 16, 384), f32),
     ]
     outs = pl.pallas_call(
         mega,
+        out_shape=[
+            jax.ShapeDtypeStruct(images.shape, b16),
+            jax.ShapeDtypeStruct(images.shape, b16),
+            jax.ShapeDtypeStruct((3, 384, 384), b16),
+            jax.ShapeDtypeStruct((16, 384), f32),
+        ],
+        in_specs=[vm, pl.BlockSpec(memory_space=pltpu.SMEM)] + [vm] * 6,
+        out_specs=[vm] * 4,
+        scratch_shapes=[pltpu.VMEM(shape, kind) for shape, kind in scratch]
+        + [
+            pltpu.SemaphoreType.DMA((5, 5)),
+            pltpu.SemaphoreType.DMA((5, 5)),
+            pltpu.SemaphoreType.DMA((6, 10)),
+            pltpu.SemaphoreType.DMA((6, 10)),
+            pltpu.SemaphoreType.DMA((10,)),
+            pltpu.SemaphoreType.DMA((10,)),
+        ],
+        compiler_params=pltpu.CompilerParams(collective_id=0, has_side_effects=True, vmem_limit_bytes=60 * 2**20),
+    )(images, counts, cotangent, pack, project_in, project_out, expand_weight, reduce_weight)
+    anywhere = pl.BlockSpec(memory_space=pl.ANY)
+    vector = jax.ShapeDtypeStruct((1, 96), f32)
+    done = pl.pallas_call(
+        finish,
         out_shape=[
             jax.ShapeDtypeStruct(images.shape, b16),
             jax.ShapeDtypeStruct(images.shape, b16),
@@ -662,26 +777,18 @@
             jax.ShapeDtypeStruct((96, 384), f32),
             jax.ShapeDtypeStruct((96, 1536), f32),
             jax.ShapeDtypeStruct((384, 384), f32),
-            jax.ShapeDtypeStruct((16, 384), f32),
-        ],
-        in_specs=[vm, pl.BlockSpec(memory_space=pltpu.SMEM)] + [vm] * 6,
-        out_specs=[vm] * 7,
-        scratch_shapes=[pltpu.VMEM(shape, kind) for shape, kind in scratch]
-        + [
-            pltpu.SemaphoreType.DMA((3, 5)),
-            pltpu.SemaphoreType.DMA((3, 5)),
-            pltpu.SemaphoreType.DMA((4, 10)),
-            pltpu.SemaphoreType.DMA((4, 10)),
-        ],
-        compiler_params=pltpu.CompilerParams(collective_id=0, has_side_effects=True, vmem_limit_bytes=60 * 2**20),
-    )(images, alive, cotangent, pack, project_in, project_out, expand_weight, reduce_weight)
-    out, ingrad, gin, gout, gexp, gred, gvec = outs
-    shard = lax.axis_index("shard")
-    part = lax.dynamic_slice(gvec, (0, shard * 96), (8, 96))
-    gbe = lax.dynamic_slice(gvec, (8 + shard, 0), (1, 384))[0]
+            jax.ShapeDtypeStruct((1, 384), f32),
+        ]
+        + [vector] * 8,
+        in_specs=[anywhere, anywhere, vm, vm],
+        out_specs=[anywhere, anywhere] + [vm] * 13,
+        scratch_shapes=[pltpu.SemaphoreType.DMA((2,))],
+        compiler_params=pltpu.CompilerParams(vmem_limit_bytes=32 * 2**20),
+    )(*outs)
+    out, ingrad, gin, gout, gexp, gred, gbe = done[:7]
+    v = [item.reshape(96) for item in done[7:]]
     return (
-        out, ingrad, part[0], part[1], gin, part[2], part[3], gout, part[4], part[5], part[6],
-        gexp, gbe, gred, part[7],
+        out, ingrad, v[0], v[1], gin, v[2], v[3], gout, v[4], v[5], v[6], gexp, gbe.reshape(384), gred, v[7],
     )
 
 

time: 104 us -> 112 us (1.077)
  Pallas kernels: 90.5 us -> 103 us
  local copies, waits for them, and re-layouts: 11.5 us -> 5.96 us
    pallas_call x1, Pallas kernels: 90.5 us -> 101 us  [fused_body(): pl.pallas_call(mega, out_shape=[jax.ShapeDtypeStruct(images.shape, b16),...]
    unnamed x34 -> x26, local copies, waits for them, and re-layouts: 8.16 us -> 5.22 us
    pallas_call x0 -> x1, Pallas kernels: none -> 2.17 us  [fused_body(): pl.pallas_call(finish, out_shape=[jax.ShapeDtypeStruct(images.shape, b16)...]
    dynamic_slice x2 -> x0, local copies, waits for them, and re-layouts: 2.08 us -> none  [the longest x1 1.31 us: fused_body(): gbe = lax.dynamic_slice(gvec, (8 + shard, 0), (1, 384))[0]]
where the time goes in v2:
time: 112 us; the launch traced here: 111 us
  Pallas kernels  103 us (92%)
  local copies, waits for them, and re-layouts  5.96 us (5%)
  between operations  1.39 us (1%)
    pallas_call x1, Pallas kernels, fused_body(): pl.pallas_call(mega, out_shape=[jax.ShapeDtypeStruct(images.shape, b16),...  101 us
    unnamed x26, local copies, waits for them, and re-layouts  5.22 us

profile of v2, /device:TPU:0, one launch (start us, length us, event | category | flops | bytes accessed | tf_op | source)
XLA Modules:
  0.0 111.4 jit_solution(17953884095228365397)
XLA Ops:
  1.3 0.0 copy-start.10
  1.3 0.0 copy-start.11
  1.3 0.0 copy-start.12
  1.3 0.0 copy-start.4
  1.3 0.0 copy-start.9
  1.3 0.7 copy-done.4
  2.0 0.0 copy-start.5
  2.0 0.0 copy-start.6
  2.0 0.0 copy-start.7
  2.0 0.0 copy-start.8
  2.0 0.1 reshape.60
  2.1 0.0 copy-done.10
  2.1 0.0 copy-done.11
  2.1 0.0 copy-done.12
  2.1 0.0 copy-done.9
  2.1 0.5 copy-done.5
  2.7 0.0 copy-done.6
  2.7 0.0 copy-done.7
  2.7 0.0 copy-done.8
  2.7 0.1 concatenate.3
  2.8 0.6 pad.4.pack_ref
  3.4 101.3 %shard_map.271 = (bf16[3,197,384]{2,1,0:T(8,128)(2,1)}, bf16[3,197,384]{2,1,0:T(8,128)(2,1)}, bf16[3,384,384]{2,1,0:T(8,128)(2,1)}, f32[16,384]{1,0:T(8,128)}) custom-call(bf16[3,197,384]{2,1,0:T(8,128)(2,1)} %images_ref.1, s32[1]{0:T(128)S(6)} %copy.31.counts_ref, bf16[3,197,384]{2,1,0:T(8,128)(2,1)} %cot_ref.1, bf16[16,128]{1,0:T(8,128)(2,1)} %pad.4.pack_ref, ...), custom_call_target="tpu_custom_call" | custom-call | tf_op jit(solution)/shard_map/pallas_call | solution.py:748
  104.7 0.0 copy-start
  104.7 1.2 %copy-done = bf16[3,384,384]{2,1,0:T(8,128)(2,1)S(1)} copy-done((bf16[3,384,384]{2,1,0:T(8,128)(2,1)S(1)}, bf16[3,384,384]{2,1,0:T(8,128)(2,1)}, u32[]{:S(2)}) %copy-start) | copy-done | bytes 884760
  105.8 0.0 copy-start.1
  105.8 1.0 copy-done.1
  106.8 0.0 copy-start.2
  106.8 1.0 copy-done.2
  107.9 0.0 copy-start.3
  107.9 0.7 copy-done.3
  108.6 2.2 %shard_map.272 = (bf16[3,197,384]{2,1,0:T(8,128)(2,1)}, bf16[3,197,384]{2,1,0:T(8,128)(2,1)}, f32[96,1152]{1,0:T(8,128)}, f32[96,384]{1,0:T(8,128)}, f32[96,1536...) custom-call(bf16[3,197,384]{2,1,0:T(8,128)(2,1)S(1)} %copy-done.1, ...), custom_call_target="tpu_custom_call" | custom-call | tf_op jit(solution)/shard_map/pallas_call | solution.py:771
  110.8 0.6 reduce
Async XLA Ops:
  1.3 0.8 copy-start.10
  1.3 0.8 copy-start.11
  1.3 0.8 copy-start.12
  1.3 0.7 copy-start.4
  1.3 0.8 copy-start.9
  2.0 0.7 copy-start.5
  2.0 0.7 copy-start.6
  2.0 0.7 copy-start.7
  2.0 0.7 copy-start.8
  104.7 1.2 %copy-start = (bf16[3,384,384]{2,1,0:T(8,128)(2,1)S(1)}, bf16[3,384,384]{2,1,0:T(8,128)(2,1)}, u32[]{:S(2)}) copy-start(bf16[3,384,384]{2,1,0:T(8,128)(2,1)} %get-tuple-element.36.sums) | copy-start | bytes 2654212
  105.8 1.0 copy-start.1
  106.8 1.0 copy-start.2
  107.9 0.7 copy-start.3

commit v3 on v1

--- a/solution.py
+++ b/solution.py
@@ -267,11 +267,11 @@
 
 
 def mega(
-    images_ref, alive_ref, cot_ref, pack_ref, win_ref, wout_ref, wexp_ref, wred_ref,
-    out_ref, ingrad_ref, gin_ref, gout_ref, gexp_ref, gred_ref, gvec_ref,
+    images_ref, counts_ref, cot_ref, pack_ref, win_ref, wout_ref, wexp_ref, wred_ref,
+    out_ref, ingrad_ref, FIN, gvec_ref,
     WI, WO, WE, WR, VG, VEC, BE,
     A1, QKV, PR, MIX, H1, XH1, XH2, RS1, RS2, A2, HID, GP, DM, DU, DH1, DZ, DMX, DT,
-    GB, AR, BS, BR, CS, CR, DR, FIN, ACC, VS, VR,
+    GB, AR, BS, BR, CS, CR, DR, ACC, VS, VR,
     gss, grs, rss, rrs,
 ):
     D = 384
@@ -305,19 +305,21 @@
         forward.append(remote(theirs, theirs, gss.at[2, k], grs.at[2, k], sib))
     for k in range(5):
         to_y[k].start()
-    for k in range(5):
         to_sib[k].start()
     for src, full, rows in items:
         full[pl.ds(pl.multiple_of(shard * rows, 16), rows), :] = src[...]
 
+    def relay(k):
+        to_y[k].wait_recv()
+        forward[k].start()
+
     def arrived(ks):
-        for k in ks:
-            to_y[k].wait_recv()
-            forward[k].start()
         for k in ks:
             to_sib[k].wait_recv()
             forward[k].wait_recv()
 
+    relay(0)
+    relay(1)
     arrived([0, 1])
     lane = lax.broadcasted_iota(jnp.int32, (128, D), 1)
     sub = lax.broadcasted_iota(jnp.int32, (128, D), 0)
@@ -332,6 +334,9 @@
     scale = HEAD_DIM ** (-0.5)
     pairs = HEADS // 2
 
+    def alive(i):
+        return jnp.where(i < counts_ref[0], 1.0, 0.0).astype(jnp.float32)
+
     def at(i):
         return pl.ds(pl.multiple_of(i * ROWS, 16), ROWS)
 
@@ -360,6 +365,15 @@
     @pl.loop(0, slots)
     def _(i):
         r = at(i)
+
+        @pl.when(i == 1)
+        def _():
+            relay(2)
+
+        @pl.when(i == 2)
+        def _():
+            relay(3)
+
         tokens = pad(images_ref[i].astype(jnp.float32))
         unit, inverse = norm(tokens)
         H1[r, :] = tokens
@@ -388,6 +402,11 @@
     @pl.loop(0, slots)
     def _(i):
         r = at(i)
+
+        @pl.when(i == 1)
+        def _():
+            relay(4)
+
         middle = H1[r, :] + mm(MIX[r, :], WO[...]) + row(4)
         H1[r, :] = middle
         unit, inverse = norm(middle)
@@ -401,7 +420,7 @@
             cdf = 0.5 * (1.0 + lax.erf(u * (0.5**0.5)))
             HID[r, cols] = (u * cdf).astype(jnp.bfloat16)
             GP[r, cols] = cdf + u * (jnp.exp(-0.5 * u * u) * 0.3989422804014327)
-        DM[r, :] = pad(cot_ref[i].astype(jnp.float32) * alive_ref[i]).astype(jnp.bfloat16)
+        DM[r, :] = pad(cot_ref[i].astype(jnp.float32) * alive(i)).astype(jnp.bfloat16)
 
     arrived([4])
     VS[...] = jnp.zeros_like(VS)
@@ -413,7 +432,7 @@
     def _(i):
         r = at(i)
         result = H1[r, :] + mm(HID[r, :], WR[...]) + row(7)
-        out_ref[i] = (result * alive_ref[i]).astype(jnp.bfloat16)[:length]
+        out_ref[i] = (result * alive(i)).astype(jnp.bfloat16)[:length]
         dm = DM[r, :]
         tally(7, dm.astype(jnp.float32))
         for s in range(4):
@@ -598,24 +617,18 @@
     vec(0)
     do_f(1)
     do_end(0)
-    gred_ref[...] = FIN[0].astype(jnp.float32)
     vec(1)
     do_c(2)
     vec(2)
     do_d(2)
     vec(3)
     do_end(1)
-    for s in range(4):
-        gexp_ref[:, s * D : s * D + D] = FIN[1, s * 96 : s * 96 + 96, :].astype(jnp.float32)
     do_e(2)
     vec(4)
     do_f(2)
     vec(5)
     gvec_ref[...] = VS[5]
     do_end(2)
-    for s in range(3):
-        gin_ref[:, s * D : s * D + D] = FIN[2, s * 96 : s * 96 + 96, :].astype(jnp.float32)
-    gout_ref[...] = FIN[2, 288:384, :].astype(jnp.float32)
 
     for k in range(5):
         to_y[k].wait_send()
@@ -630,12 +643,41 @@
         step_f(n).wait_send()
 
 
+def finish(
+    out_in, ingrad_in, sums, vectors, out_ref, ingrad_ref, gin_ref, gout_ref, gexp_ref, gred_ref, gbe_ref, *rest
+):
+    D = 384
+    vector_refs, sem = rest[:8], rest[8]
+    copies = [
+        pltpu.make_async_copy(out_in, out_ref, sem.at[0]),
+        pltpu.make_async_copy(ingrad_in, ingrad_ref, sem.at[1]),
+    ]
+    for copy in copies:
+        copy.start()
+    shard = lax.axis_index("shard")
+    mine, expand = jnp.zeros((8, 96), jnp.float32), jnp.zeros((1, D), jnp.float32)
+    for s in range(4):
+        chosen = jnp.where(shard == s, 1.0, 0.0).astype(jnp.float32)
+        mine = mine + chosen * vectors[0:8, s * 96 : s * 96 + 96]
+        expand = expand + chosen * vectors[8 + s : 9 + s, :]
+    for j in range(8):
+        vector_refs[j][...] = mine[j : j + 1, :]
+    gbe_ref[...] = expand
+    gred_ref[...] = sums[0].astype(jnp.float32)
+    for s in range(4):
+        gexp_ref[:, s * D : s * D + D] = sums[1, s * 96 : s * 96 + 96, :].astype(jnp.float32)
+    for s in range(3):
+        gin_ref[:, s * D : s * D + D] = sums[2, s * 96 : s * 96 + 96, :].astype(jnp.float32)
+    gout_ref[...] = sums[2, 288:384, :].astype(jnp.float32)
+    for copy in copies:
+        copy.wait()
+
+
 def fused_body(
     images, counts, first_gain, first_shift, project_in, query_bias, value_bias, project_out, output_bias,
     second_gain, second_shift, expand_weight, expand_bias, reduce_weight, reduce_bias, cotangent,
 ):
     slots, length, width = images.shape
-    alive = (jnp.arange(slots) < counts[0]).astype(jnp.float32)
     rows = [first_gain, first_shift, query_bias, value_bias, output_bias, second_gain, second_shift, reduce_bias]
     pack = jnp.concatenate([jnp.stack(rows), expand_bias.reshape(4, 96)], axis=0)
     pack = jnp.pad(pack, ((0, 4), (0, 32)))
@@ -650,7 +692,7 @@
         ((n, 1536), f32), ((n, 384), b16), ((n, 1536), b16), ((n, 384), f32), ((n, 384), b16), ((n, 384), b16),
         ((n, 1152), b16),
         ((3, 2, 2, 384, 384), b16), ((3, 2, 384, 384), b16), ((3, 384, 384), b16), ((3, 384, 384), b16),
-        ((3, 384, 384), b16), ((3, 192, 384), b16), ((3, 3, 48, 384), b16), ((3, 384, 384), b16), ((3, 384, 384), f32),
+        ((3, 384, 384), b16), ((3, 192, 384), b16), ((3, 3, 48, 384), b16), ((3, 384, 384), f32),
         ((6, 16, 384), f32), ((5, 16, 384), f32),
     ]
     outs = pl.pallas_call(
@@ -658,14 +700,11 @@
         out_shape=[
             jax.ShapeDtypeStruct(images.shape, b16),
             jax.ShapeDtypeStruct(images.shape, b16),
-            jax.ShapeDtypeStruct((96, 1152), f32),
-            jax.ShapeDtypeStruct((96, 384), f32),
-            jax.ShapeDtypeStruct((96, 1536), f32),
-            jax.ShapeDtypeStruct((384, 384), f32),
+            jax.ShapeDtypeStruct((3, 384, 384), b16),
             jax.ShapeDtypeStruct((16, 384), f32),
         ],
         in_specs=[vm, pl.BlockSpec(memory_space=pltpu.SMEM)] + [vm] * 6,
-        out_specs=[vm] * 7,
+        out_specs=[vm] * 4,
         scratch_shapes=[pltpu.VMEM(shape, kind) for shape, kind in scratch]
         + [
             pltpu.SemaphoreType.DMA((3, 5)),
@@ -674,14 +713,30 @@
             pltpu.SemaphoreType.DMA((4, 10)),
         ],
         compiler_params=pltpu.CompilerParams(collective_id=0, has_side_effects=True, vmem_limit_bytes=60 * 2**20),
-    )(images, alive, cotangent, pack, project_in, project_out, expand_weight, reduce_weight)
-    out, ingrad, gin, gout, gexp, gred, gvec = outs
-    shard = lax.axis_index("shard")
-    part = lax.dynamic_slice(gvec, (0, shard * 96), (8, 96))
-    gbe = lax.dynamic_slice(gvec, (8 + shard, 0), (1, 384))[0]
+    )(images, counts, cotangent, pack, project_in, project_out, expand_weight, reduce_weight)
+    anywhere = pl.BlockSpec(memory_space=pl.ANY)
+    vector = jax.ShapeDtypeStruct((1, 96), f32)
+    done = pl.pallas_call(
+        finish,
+        out_shape=[
+            jax.ShapeDtypeStruct(images.shape, b16),
+            jax.ShapeDtypeStruct(images.shape, b16),
+            jax.ShapeDtypeStruct((96, 1152), f32),
+            jax.ShapeDtypeStruct((96, 384), f32),
+            jax.ShapeDtypeStruct((96, 1536), f32),
+            jax.ShapeDtypeStruct((384, 384), f32),
+            jax.ShapeDtypeStruct((1, 384), f32),
+        ]
+        + [vector] * 8,
+        in_specs=[anywhere, anywhere, vm, vm],
+        out_specs=[anywhere, anywhere] + [vm] * 13,
+        scratch_shapes=[pltpu.SemaphoreType.DMA((2,))],
+        compiler_params=pltpu.CompilerParams(vmem_limit_bytes=60 * 2**20),
+    )(*outs)
+    out, ingrad, gin, gout, gexp, gred, gbe = done[:7]
+    v = [item.reshape(96) for item in done[7:]]
     return (
-        out, ingrad, part[0], part[1], gin, part[2], part[3], gout, part[4], part[5], part[6],
-        gexp, gbe, gred, part[7],
+        out, ingrad, v[0], v[1], gin, v[2], v[3], gout, v[4], v[5], v[6], gexp, gbe.reshape(384), gred, v[7],
     )
 
 

time: 104 us -> 128 us (1.23)
  Pallas kernels: 90.5 us -> 123 us
  local copies, waits for them, and re-layouts: 11.5 us -> 2.7 us
    pallas_call x0 -> x1, Pallas kernels: none -> 31.5 us  [fused_body(): pl.pallas_call(finish, out_shape=[jax.ShapeDtypeStruct(images.shape, b16)...]
    unnamed x34 -> x20, local copies, waits for them, and re-layouts: 8.16 us -> 1.96 us
    dynamic_slice x2 -> x0, local copies, waits for them, and re-layouts: 2.08 us -> none  [the longest x1 1.31 us: fused_body(): gbe = lax.dynamic_slice(gvec, (8 + shard, 0), (1, 384))[0]]
where the time goes in v3:
time: 128 us; the launch traced here: 127 us
  Pallas kernels  123 us (96%)
  local copies, waits for them, and re-layouts  2.7 us (2%)
  between operations  1.38 us (1%)
    pallas_call x1, Pallas kernels, fused_body(): pl.pallas_call(mega, out_shape=[jax.ShapeDtypeStruct(images.shape, b16),...  91.2 us
    pallas_call x1, Pallas kernels, fused_body(): pl.pallas_call(finish, out_shape=[jax.ShapeDtypeStruct(images.shape, b16)...  31.5 us

profile of v3, /device:TPU:0, one launch (start us, length us, event | category | flops | bytes accessed | tf_op | source)
XLA Modules:
  0.0 127.4 jit_solution(12730344820157865451)
XLA Ops:
  1.3 0.0 copy-start.7
  1.3 0.0 copy-start.8
  1.3 0.0 copy-start.9
  1.3 0.0 copy-start.1
  1.3 0.0 copy-start.6
  1.3 0.7 copy-done.1
  2.0 0.0 copy-start.2
  2.0 0.0 copy-start.3
  2.0 0.0 copy-start.4
  2.0 0.0 copy-start.5
  2.0 0.1 reshape.60
  2.1 0.0 copy-done.7
  2.1 0.0 copy-done.8
  2.1 0.0 copy-done.9
  2.1 0.0 copy-done.6
  2.1 0.5 copy-done.2
  2.7 0.0 copy-done.3
  2.7 0.0 copy-done.4
  2.7 0.0 copy-done.5
  2.7 0.1 concatenate.3
  2.8 0.6 pad.4.pack_ref
  3.4 91.2 %shard_map.271 = (bf16[3,197,384]{2,1,0:T(8,128)(2,1)}, bf16[3,197,384]{2,1,0:T(8,128)(2,1)}, bf16[3,384,384]{2,1,0:T(8,128)(2,1)}, f32[16,384]{1,0:T(8,128)}) custom-call(bf16[3,197,384]{2,1,0:T(8,128)(2,1)} %images_ref.1, s32[1]{0:T(128)S(6)} %copy.31.counts_ref, bf16[3,197,384]{2,1,0:T(8,128)(2,1)} %cot_ref.1, bf16[16,128]{1,0:T(8,128)(2,1)} %pad.4.pack_ref, ...), custom_call_target="tpu_custom_call" | custom-call | tf_op jit(solution)/shard_map/pallas_call | solution.py:698
  94.6 31.5 %shard_map.272 = (bf16[3,197,384]{2,1,0:T(8,128)(2,1)}, bf16[3,197,384]{2,1,0:T(8,128)(2,1)}, f32[96,1152]{1,0:T(8,128)}, f32[96,384]{1,0:T(8,128)}, f32[96,1536...) custom-call(bf16[3,197,384]{2,1,0:T(8,128)(2,1)} %get-tuple-element., ...), custom_call_target="tpu_custom_call" | custom-call | tf_op jit(solution)/shard_map/pallas_call | solution.py:719
  126.1 0.0 copy-start
  126.1 0.7 copy-done
  126.8 0.6 reduce
Async XLA Ops:
  1.3 0.8 copy-start.7
  1.3 0.8 copy-start.8
  1.3 0.8 copy-start.9
  1.3 0.7 copy-start.1
  1.3 0.8 copy-start.6
  2.0 0.7 copy-start.2
  2.0 0.7 copy-start.3
  2.0 0.7 copy-start.4
  2.0 0.7 copy-start.5
  126.1 0.7 copy-start
